TPU v7x, 32 devices: a whole 2x2x4 slice. The times are simulated.
32 devices in a mesh: gx: 4 (over z), gy: 4 (over x, core), gz: 2 (over y).
Axes of the slice: x: 2, y: 2, z: 4, core: 2. Of those that a mesh axis runs over, the one named last changes fastest.
Arguments:
- phases: float32 [16, 16, 2, 96, 256], P('gx', 'gy', 'gz'), may hold values from -3.140625 to 3.140625
- diag_tiles: float32 [16, 16, 2, 96, 96], P('gx', 'gy', 'gz'), may hold values from -0.078125 to 0.078125
- local_tiles: float32 [4, 4, 2, 48, 96, 96], P('gx', 'gy', 'gz'), may hold values from -0.078125 to 0.078125
- local_pairs: int32 [4, 4, 2, 2, 48], P('gx', 'gy', 'gz'), may hold values from 0 to 15
- face_tiles: float32 [4, 4, 2, 2, 8, 96, 96], P('gx', 'gy', 'gz'), may hold values from -0.078125 to 0.078125
- face_pairs: int32 [4, 4, 2, 2, 2, 8], P('gx', 'gy', 'gz'), may hold values from 0 to 3
- layer_tiles: float32 [4, 4, 2, 32, 96, 96], P('gx', 'gy', 'gz'), may hold values from -0.078125 to 0.078125
- layer_pairs: int32 [4, 4, 2, 2, 32], P('gx', 'gy', 'gz'), may hold values from 0 to 15
Outputs:
- order_three: float32 [16, 16, 2, 96, 256], P('gx', 'gy', 'gz')
- moments: float32 [2, 7, 256], P('gz')
Inputs may be any that keep to these rules, and one draw needn't show every extreme that they name: `local_pairs`: local pairs may repeat and may name one cluster twice. `face_pairs`: face slots number clusters along the face.
All inputs are finite; a program needn't handle non-finite values.
Results may differ from a plain program's by a relative error of at most 0.00005.
Values sent between devices are 32-bit elements; how exact they have to be, the bound alone decides.
A program may use at most 128 MiB of HBM per device.

v0:
```python
import functools
import math

import jax
import jax.numpy as jnp
from jax import lax
from jax.experimental import pallas as pl
from jax.experimental.pallas import tpu as pltpu
from jax.sharding import PartitionSpec as P

CHUNKS = 2
MESH = pl.DeviceIdType.MESH
VMEM_LIMIT = 60 * 1024 * 1024


def passed_along(block, axis, distance):
    count = lax.axis_size(axis)
    route = [((i - distance) % count, i) for i in range(count)]
    return lax.ppermute(block, axis, route)


def halves(values):
    high = values.astype(jnp.bfloat16)
    return high, (values - high.astype(jnp.float32)).astype(jnp.bfloat16)


def build_kernel(plan, edge, *refs):
    n_src = 1 + max(source for _, parts in plan for source, _ in parts)
    pairs, tiles = refs[:n_src], refs[n_src : 2 * n_src]
    outs = refs[2 * n_src : 2 * n_src + len(plan)]
    block, wide, turn = refs[2 * n_src + len(plan) :]
    degrees, slab = wide.shape
    wide[...] = jnp.zeros_like(wide)
    turn[...] = jnp.zeros_like(turn)

    def place(row, column, span, values):
        wide[:, 0 : values.shape[1]] = values
        group, slot = column // edge, column % edge
        moved = pltpu.roll(wide[...], slot * degrees, 1)
        start = pl.multiple_of(group * slab, slab)
        block[row, :, pl.ds(start, slab)] += moved

    for out, (clusters, parts) in zip(outs, plan):
        span = clusters * degrees

        def clear(i, carry):
            block[i, :, 0:span] = jnp.zeros((degrees, span), jnp.float32)
            return carry

        lax.fori_loop(0, clusters, clear, 0)
        for source, kind in parts:

            def one(k, carry, source=source, kind=kind):
                if kind == "diagonal":
                    first, second = k, k
                else:
                    first, second = pairs[source][0, k], pairs[source][1, k]
                tile = tiles[source][k]
                if kind != "reverse":
                    place(first, second, span, tile)
                if kind != "forward":
                    turn[0:degrees, 0:degrees] = tile
                    place(second, first, span, turn[...].T[0:degrees])
                return carry

            lax.fori_loop(0, tiles[source].shape[0], one, 0)

        def write(i, carry, out=out, span=span):
            high, low = halves(block[i, :, 0:span])
            group, at = i // edge, pl.multiple_of((i % edge) * degrees, degrees)
            out[group, pl.ds(at, degrees), :] = high
            out[group, pl.ds(slab + at, degrees), :] = low
            return carry

        lax.fori_loop(0, clusters, write, 0)


def build(plan, edge, pairs, tiles):
    degrees = tiles[0].shape[-1]
    slab = edge * degrees
    most = max(clusters for clusters, _ in plan)
    around = -(-degrees // 128) * 128
    return pl.pallas_call(
        functools.partial(build_kernel, plan, edge),
        out_shape=[
            jax.ShapeDtypeStruct((c // edge, 2 * slab, c * degrees), jnp.bfloat16) for c, _ in plan
        ],
        in_specs=[pl.BlockSpec(memory_space=pltpu.SMEM)] * len(pairs)
        + [pl.BlockSpec(memory_space=pltpu.VMEM)] * len(tiles),
        out_specs=[pl.BlockSpec(memory_space=pltpu.VMEM)] * len(plan),
        scratch_shapes=[
            pltpu.VMEM((most, degrees, most * degrees), jnp.float32),
            pltpu.VMEM((degrees, slab), jnp.float32),
            pltpu.VMEM((around, around), jnp.float32),
        ],
        compiler_params=pltpu.CompilerParams(vmem_limit_bytes=VMEM_LIMIT),
        cost_estimate=pl.CostEstimate(flops=10**7, bytes_accessed=10**7, transcendentals=0),
    )(*pairs, *tiles)


def recur_kernel(layers, width_x, width_y, normalizer, *refs):
    ways = min(layers - 1, 2)
    field0, first_layer = refs[0], refs[1 : 1 + ways]
    first_faces, refs = refs[1 + ways : 5 + ways], refs[5 + ways :]
    own, across, sides, refs = refs[0], refs[1 : 1 + ways], refs[1 + ways : 5 + ways], refs[5 + ways :]
    out, moments, field1, field2, field3, got_layer, got_face, refs = *refs[:7], refs[7:]
    split, split_side, partial, got_y, got_x, send_sem, recv_sem, sum_send, sum_recv = refs
    chunks, edge, _, degrees, width = field0.shape
    slab = edge * degrees
    fields = [field0, field1, field2, field3]
    me_x, me_y, me_z = lax.axis_index("gx"), lax.axis_index("gy"), lax.axis_index("gz")
    x_peers = [{"gx": lax.rem(me_x + d, width_x)} for d in range(1, width_x)]
    y_peers = [{"gy": lax.rem(me_y + d, width_y)} for d in range(1, width_y)]
    below = {"gz": lax.rem(me_z + layers - 1, layers)}
    above = {"gz": lax.rem(me_z + 1, layers)}
    z_peers = [below, above][:ways]

    barrier = pltpu.get_barrier_semaphore()
    for peer in x_peers + y_peers + z_peers:
        pl.semaphore_signal(barrier, inc=1, device_id=peer, device_id_type=MESH)
    pl.semaphore_wait(barrier, len(x_peers) + len(y_peers) + ways)

    def copies(op, ch):
        field = fields[op + 1]
        found = []
        for j in range(ways):
            found.append((field.at[ch], got_layer.at[op, j, ch], z_peers[j]))
        ends = [
            (field.at[ch, 0], x_peers[-1]),
            (field.at[ch, edge - 1], x_peers[0]),
            (field.at[ch, :, 0], y_peers[-1]),
            (field.at[ch, :, edge - 1], y_peers[0]),
        ]
        for j, (source, peer) in enumerate(ends):
            found.append((source, got_face.at[op, j, ch], peer))
        order = found[ways:] + found[:ways]
        return [
            pltpu.make_async_remote_copy(
                src_ref=source,
                dst_ref=target,
                send_sem=send_sem.at[op, ch, j],
                recv_sem=recv_sem.at[op, ch, j],
                device_id=peer,
                device_id_type=MESH,
            )
            for j, (source, target, peer) in enumerate(order)
        ]

    def into_split(values, i):
        high, low = halves(values.reshape(slab, width))
        split[pl.ds(pl.multiple_of(i * slab, slab), slab), 0:width] = high
        split[pl.ds(pl.multiple_of(i * slab, slab), slab), width : 2 * width] = low

    def folded(both):
        four = both[0:slab] + both[slab : 2 * slab]
        return four[:, 0:width] + four[:, width : 2 * width]

    def apply(matrix, source, target, ch, fresh):
        def fill(i, carry):
            into_split(source(i), i)
            return carry

        lax.fori_loop(0, edge, fill, 0)

        def part(i, carry):
            both = jnp.dot(matrix[i], split[...], preferred_element_type=jnp.float32)
            value = folded(both).reshape(edge, degrees, width)
            target[ch, i] = value if fresh else target[ch, i] + value
            return carry

        lax.fori_loop(0, edge, part, 0)

    def side(j, values):
        high, low = halves(values.reshape(slab, width))
        split_side[:, 0:width] = high
        split_side[:, width : 2 * width] = low
        both = jnp.dot(sides[j][0], split_side[...], preferred_element_type=jnp.float32)
        return folded(both).reshape(edge, degrees, width)

    def inner(left, right, ch):
        def add(i, total):
            return total + jnp.sum(
                (left[ch, i] * right[ch, i]).reshape(slab, width), axis=0, keepdims=True
            )

        return lax.fori_loop(0, edge, add, jnp.zeros((1, width), jnp.float32))

    partial[...] = jnp.zeros_like(partial)
    for op in range(3):
        field, target = fields[op], fields[op + 1]

        def step(ch, carry, op=op, field=field, target=target):
            apply(own, lambda i: field[ch, i], target, ch, True)
            if op > 0:
                for copy in copies(op - 1, ch):
                    copy.wait_recv()
            for j in range(ways):
                if op == 0:
                    apply(across[j], lambda i: first_layer[j][ch, i], target, ch, False)
                else:
                    apply(across[j], lambda i: got_layer[op - 1, j, ch, i], target, ch, False)
            face = [
                first_faces[j][ch] if op == 0 else got_face[op - 1, j, ch] for j in range(4)
            ]
            target[ch, edge - 1] += side(0, face[0])
            target[ch, 0] += side(1, face[1])
            target[ch, :, edge - 1] += side(2, face[2])
            target[ch, :, 0] += side(3, face[3])
            if op > 0:

                def combine(i, carry):
                    target[ch, i] = 2.0 * target[ch, i] - fields[op - 1][ch, i]
                    return carry

                lax.fori_loop(0, edge, combine, 0)
            if op < 2:
                for copy in copies(op, ch):
                    copy.start()
            if op == 0:
                partial[ch, 0:1] = inner(field, field, ch)
            partial[ch, 2 * op + 1 : 2 * op + 2] = inner(target, field, ch)
            partial[ch, 2 * op + 2 : 2 * op + 3] = inner(target, target, ch)
            return carry

        lax.fori_loop(0, chunks, step, 0)

    def gather(stage, peers, slots):
        sends = [
            pltpu.make_async_remote_copy(
                src_ref=partial.at[:],
                dst_ref=slots.at[d],
                send_sem=sum_send.at[stage, d],
                recv_sem=sum_recv.at[stage, d],
                device_id=peer,
                device_id_type=MESH,
            )
            for d, peer in enumerate(peers)
        ]
        for send in sends:
            send.start()
        return sends

    sends = gather(0, y_peers, got_y)
    for ch in range(chunks):
        out[:, :, 0, :, ch * width : (ch + 1) * width] = field3[ch]
    for send in sends:
        send.wait()
    total = partial[...]
    for d in range(len(y_peers)):
        total = total + got_y[d]
    partial[...] = total
    sends = gather(1, x_peers, got_x)
    for send in sends:
        send.wait()
    total = partial[...]
    for d in range(len(x_peers)):
        total = total + got_x[d]
    total = total * (1.0 / normalizer)
    for ch in range(chunks):
        at = slice(ch * width, (ch + 1) * width)
        for k in range(7):
            row = total[ch, k : k + 1]
            if k > 1:
                row = 2.0 * row - total[ch, k % 2 : k % 2 + 1]
            moments[0, k : k + 1, at] = row

    for op in range(2):

        def finish(ch, carry, op=op):
            for copy in copies(op, ch):
                copy.wait_send()
            return carry

        lax.fori_loop(0, chunks, finish, 0)


def recur(field, layer_fields, face_fields, own, across, sides, out_shape, normalizer):
    chunks, edge, _, degrees, width = field.shape
    layers, nx, ny = lax.axis_size("gz"), lax.axis_size("gx"), lax.axis_size("gy")
    ways = len(layer_fields)
    operands = [field, *layer_fields, *face_fields, own, *across, *sides]
    f32 = jnp.float32
    rows = edge * edge * degrees
    return pl.pallas_call(
        functools.partial(recur_kernel, layers, nx, ny, normalizer),
        out_shape=[
            jax.ShapeDtypeStruct(out_shape, f32),
            jax.ShapeDtypeStruct((1, 7, chunks * width), f32),
        ],
        in_specs=[pl.BlockSpec(memory_space=pltpu.VMEM)] * len(operands),
        out_specs=[pl.BlockSpec(memory_space=pltpu.VMEM)] * 2,
        scratch_shapes=[
            pltpu.VMEM(field.shape, f32),
            pltpu.VMEM(field.shape, f32),
            pltpu.VMEM(field.shape, f32),
            pltpu.VMEM((2, ways) + field.shape, f32),
            pltpu.VMEM((2, 4, chunks, edge, degrees, width), f32),
            pltpu.VMEM((rows, 2 * width), jnp.bfloat16),
            pltpu.VMEM((edge * degrees, 2 * width), jnp.bfloat16),
            pltpu.VMEM((chunks, 8, width), f32),
            pltpu.VMEM((ny - 1, chunks, 8, width), f32),
            pltpu.VMEM((nx - 1, chunks, 8, width), f32),
            pltpu.SemaphoreType.DMA((2, chunks, ways + 4)),
            pltpu.SemaphoreType.DMA((2, chunks, ways + 4)),
            pltpu.SemaphoreType.DMA((2, max(nx, ny) - 1)),
            pltpu.SemaphoreType.DMA((2, max(nx, ny) - 1)),
        ],
        compiler_params=pltpu.CompilerParams(
            collective_id=0, has_side_effects=True, vmem_limit_bytes=VMEM_LIMIT
        ),
    )(*operands)


def shards(
    phases, diag_tiles, local_tiles, local_pairs, face_tiles, face_pairs, layer_tiles, layer_pairs
):
    edge = phases.shape[0]
    clusters = edge * edge
    degrees, columns = phases.shape[3:]
    layers = lax.axis_size("gz")
    width = columns // CHUNKS

    own_layer, own_layer_pairs = layer_tiles[0, 0, 0], layer_pairs[0, 0, 0]
    faces, face_places = face_tiles[0, 0, 0], face_pairs[0, 0, 0]
    below_set = passed_along(own_layer, "gz", 1)
    below_pairs = passed_along(own_layer_pairs, "gz", 1)
    west_set = passed_along(faces[0], "gx", 1)
    west_pairs = passed_along(face_places[0], "gx", 1)
    south_set = passed_along(faces[1], "gy", 1)
    south_pairs = passed_along(face_places[1], "gy", 1)

    initial = math.sqrt(2.0) * jnp.cos(phases[:, :, 0])
    field = jnp.stack([initial[..., i * width : (i + 1) * width] for i in range(CHUNKS)])
    layer_fields = [passed_along(field, "gz", -1)]
    if layers > 2:
        layer_fields.append(passed_along(field, "gz", 1))
    face_fields = [
        passed_along(field[:, 0], "gx", -1),
        passed_along(field[:, edge - 1], "gx", 1),
        passed_along(field[:, :, 0], "gy", -1),
        passed_along(field[:, :, edge - 1], "gy", 1),
    ]

    diagonal = diag_tiles.reshape(clusters, degrees, degrees)
    own, east, north = build(
        [
            (clusters, [(0, "both"), (3, "diagonal")]),
            (edge, [(1, "forward")]),
            (edge, [(2, "forward")]),
        ],
        edge,
        [local_pairs[0, 0, 0], face_places[0], face_places[1], face_places[0]],
        [local_tiles[0, 0, 0], faces[0], faces[1], diagonal],
    )
    if layers > 2:
        layer_plan = [(clusters, [(0, "forward")]), (clusters, [(1, "reverse")])]
    else:
        layer_plan = [(clusters, [(0, "forward"), (1, "reverse")])]
    *across, west, south = build(
        layer_plan + [(edge, [(2, "reverse")]), (edge, [(3, "reverse")])],
        edge,
        [own_layer_pairs, below_pairs, west_pairs, south_pairs],
        [own_layer, below_set, west_set, south_set],
    )
    normalizer = lax.axis_size("gx") * lax.axis_size("gy") * clusters * degrees
    order_three, moments = recur(
        field,
        layer_fields,
        face_fields,
        own,
        across,
        [east, west, north, south],
        (edge, edge, 1, degrees, columns),
        float(normalizer),
    )
    return order_three, moments


def solution(mesh):
    in_specs = (
        P("gx", "gy", "gz", None, None),
        P("gx", "gy", "gz", None, None),
        P("gx", "gy", "gz", None, None, None),
        P("gx", "gy", "gz", None, None),
        P("gx", "gy", "gz", None, None, None, None),
        P("gx", "gy", "gz", None, None, None),
        P("gx", "gy", "gz", None, None, None),
        P("gx", "gy", "gz", None, None),
    )
    out_specs = (P("gx", "gy", "gz", None, None), P("gz", None, None))
    return jax.shard_map(shards, mesh=mesh, in_specs=in_specs, out_specs=out_specs, check_vma=False)
```

profile of v0, /device:TPU:0, one launch (start us, length us, event | category | flops | bytes accessed | tf_op | source)
XLA Modules:
  0.0 247.3 jit_solution(1883101489436896751)
XLA Ops:
  0.6 6.1 %fusion.1 = f32[4,4,96,256]{3,2,0,1:T(8,128)S(1)} fusion(f32[4,4,1,96,256]{4,3,2,1,0:T(8,128)} %param.8), kind=kLoop, calls=%fused_computation.11 | loop fusion | flops 393216 | bytes 3145728 | tf_op jit(solution)/shard_map/mul | solution.py:332
  6.7 0.2 slice_bitcast_fusion.1
  6.9 0.0 copy-start
  6.9 0.0 copy-start.10
  7.0 0.0 copy-start.11
  7.0 0.2 pad_maximum_fusion
  7.1 0.0 copy-start.3
  7.1 3.0 %collective-permute-start = (f32[2,4,4,96,128]{4,3,1,0,2:T(8,128)S(1)}, f32[2,4,4,96,128]{4,3,1,0,2:T(8,128)}, u32[]{:S(2)}, u32[]{:S(2)}) collective-permute-start(f32[2,4,4,96,128]{4,3,1,0,2:T(8,128)S(1)} %pad_maximum_fusion), channel_id=1, source_target_pairs={{1,0},{0,1},{3,2},{2,3},{5,4},{4,5},{7,6},{6,7},{9,8},{8,9},{11,10... | collective-permute-start | bytes 4718600 | tf_op jit(solution)/shard_map/ppermute | solution.py:19
  10.2 1.1 collective-permute-start.8
  11.3 0.1 collective-permute-start.7
  11.4 1.6 collective-permute-start.6
  13.0 0.9 collective-permute-start.5
  13.9 0.1 fusion.5
  14.0 0.4 collective-permute-done.7.refs_3_
  14.4 1.6 collective-permute-start.2
  16.0 0.9 collective-permute-done.6.refs_2_
  16.8 1.8 collective-permute-start.1
  18.6 0.1 slice_bitcast_fusion.2
  18.7 0.0 copy-done.8
  18.7 0.0 copy-done.9
  18.7 0.0 copy-start.1
  18.7 0.0 copy-start.2
  18.7 59.7 %collective-permute-done.5.refs_1_ = s32[2,32]{1,0:T(2,128)S(1)} collective-permute-done((s32[2,32]{1,0:T(2,128)S(1)}, s32[2,32]{1,0:T(2,128)S(1)}, u32[]{:S(2)}, u32[]{:S(2)}) %collective-permute-start.5) | collective-permute-done | bytes 288 | tf_op jit(solution)/shard_map/ppermute | solution.py:19
  78.4 0.0 collective-permute-start.10
  78.4 1.0 fusion.9
  79.4 0.0 copy-done.12
  79.4 6.2 %collective-permute-done.10.refs_7_ = f32[8,96,96]{2,1,0:T(8,128)S(1)} collective-permute-done((f32[8,96,96]{2,1,0:T(8,128)S(1)}, f32[8,96,96]{2,1,0:T(8,128)S(1)}, u32[]{:S(2)}, u32[]{:S(2)}) %collective-permute-start.10) | collective-permute-done | bytes 294944 | tf_op jit(solution)/shard_map/ppermute | solution.py:19
  85.6 0.0 collective-permute-start.4
  85.6 0.0 collective-permute-done.2
  85.6 1.7 collective-permute-start.3
  87.4 0.0 collective-permute-done.1
  87.4 0.8 copy-done.7
  88.1 1.8 collective-permute-start.9
  89.9 1.3 copy.12.refs_0_
  91.2 25.7 %shard_map.95 = (bf16[4,768,1536]{2,1,0:T(8,128)(2,1)}, bf16[1,768,384]{2,1,0:T(8,128)(2,1)}, bf16[1,768,384]{2,1,0:T(8,128)(2,1)}) custom-call(s32[2,48]{1,0:T(2,128)} %bitcast.33, s32[2,8]{1,0:T(2,128)} %copy-done.8, s32[2,8]{1,0:T(2,128)} %copy-done.9, s32[2,8]{1,0:T(2,128)} %copy-done.8, f32[48,96,96]{2,1,0:T(8,128)} %bitcast.29, ...), custom_call_target="tpu_custom_call" | custom-call | flops 10000000 | bytes 10000000 | tf_op jit(solution)/shard_map/pallas_call | solution.py:83
  116.9 0.0 copy-done.6
  116.9 0.8 copy.15.refs_3_
  117.7 1.8 copy.14.refs_2_
  119.5 0.0 collective-permute-done.9.refs_6_
  119.5 0.0 collective-permute-done.8.refs_5_
  119.5 20.8 %shard_map.96 = (bf16[4,768,1536]{2,1,0:T(8,128)(2,1)}, bf16[1,768,384]{2,1,0:T(8,128)(2,1)}, bf16[1,768,384]{2,1,0:T(8,128)(2,1)}) custom-call(s32[2,32]{1,0:T(2,128)} %bitcast.34, s32[2,32]{1,0:T(2,128)} %copy-done.14, s32[2,8]{1,0:T(2,128)} %copy-done.13, s32[2,8]{1,0:T(2,128)} %copy-done.12, f32[32,96,96]{2,1,0:T(8,128)} %bitcast.30, ...), custom_call_target="tpu_custom_call" | custom-call | flops 10000000 | bytes 10000000 | tf_op jit(solution)/shard_map/pallas_call | solution.py:83
  140.3 0.0 collective-permute-done
  140.3 2.7 %copy.13.refs_1_ = f32[2,4,4,96,128]{4,3,2,1,0:T(8,128)} copy(f32[2,4,4,96,128]{4,3,1,0,2:T(8,128)} %collective-permute-done) | data formatting | bytes 3145728 | tf_op jit(solution)/shard_map/ppermute | solution.py:19
  143.0 0.0 collective-permute-done.4.refs_5_
  143.0 0.0 collective-permute-done.3.refs_4_
  143.0 100.3 %shard_map.97 = (f32[4,4,1,96,256]{4,3,2,1,0:T(8,128)}, f32[1,7,256]{2,1,0:T(8,128)}) custom-call(f32[2,4,4,96,128]{4,3,2,1,0:T(8,128)} %copy.12.refs_0_, f32[2,4,4,96,128]{4,3,2,1,0:T(8,128)} %copy.13.refs_1_, f32[2,4,96,128]{3,2,1,0:T(8,128)} %copy.14.refs_2_, f32[2,4,96,128]{3,2,1,0:T(8,128)} %copy.15.refs_3_, ...), custom_call_target="tpu_custom_call" | custom-call | tf_op jit(solution)/shard_map/pallas_call | solution.py:284
  243.4 1.3 copy.16
  244.7 2.7 %copy.23 = f32[4,4,1,96,256]{4,3,2,1,0:T(8,128)} copy(f32[4,4,1,96,256]{4,3,2,1,0:T(8,128)} %get-tuple-element.28) | data formatting | bytes 3145728
  (20 shorter events, 0.0 us)
Async XLA Ops:
  6.9 3.2 %copy-start = (f32[1,1,1,32,96,96]{5,4,3,2,1,0:T(8,128)S(1)}, f32[1,1,1,32,96,96]{5,4,3,2,1,0:T(8,128)}, u32[]{:S(2)}) copy-start(f32[1,1,1,32,96,96]{5,4,3,2,1,0:T(8,128)} %param.14) | copy-start | bytes 3538948
  6.9 4.4 %copy-start.10 = (s32[1,1,1,2,2,8]{5,4,3,2,1,0:T(2,128)S(1)}, s32[1,1,1,2,2,8]{5,4,3,2,1,0:T(2,128)}, u32[]{:S(2)}) copy-start(s32[1,1,1,2,2,8]{5,4,3,2,1,0:T(2,128)} %param.13) | copy-start | bytes 388
  7.0 6.1 %copy-start.11 = (s32[1,1,1,2,32]{4,3,2,1,0:T(2,128)S(1)}, s32[1,1,1,2,32]{4,3,2,1,0:T(2,128)}, u32[]{:S(2)}) copy-start(s32[1,1,1,2,32]{4,3,2,1,0:T(2,128)} %param.15) | copy-start | bytes 772
  7.1 11.5 %copy-start.3 = (f32[1,1,1,2,8,96,96]{6,5,4,3,2,1,0:T(8,128)S(1)}, f32[1,1,1,2,8,96,96]{6,5,4,3,2,1,0:T(8,128)}, u32[]{:S(2)}) copy-start(f32[1,1,1,2,8,96,96]{6,5,4,3,2,1,0:T(8,128)} %param.12) | copy-start | bytes 1769476
  7.1 133.2 %collective-permute-start = (f32[2,4,4,96,128]{4,3,1,0,2:T(8,128)S(1)}, f32[2,4,4,96,128]{4,3,1,0,2:T(8,128)}, u32[]{:S(2)}, u32[]{:S(2)}) collective-permute-start(f32[2,4,4,96,128]{4,3,1,0,2:T(8,128)S(1)} %pad_maximum_fusion), channel_id=1, source_target_pairs={{1,0},{0,1},{3,2},{2,3},{5,4},{4,5},{7,6},{6,7},{9,8},{8,9},{11,10... | collective-permute-start | bytes 4718600 | tf_op jit(solution)/shard_map/ppermute | solution.py:19
  10.2 109.3 %collective-permute-start.8 = (f32[32,96,96]{2,1,0:T(8,128)S(1)}, f32[32,96,96]{2,1,0:T(8,128)}, u32[]{:S(2)}, u32[]{:S(2)}) collective-permute-start(f32[32,96,96]{2,1,0:T(8,128)S(1)} %bitcast.31), channel_id=1, source_target_pairs={{1,0},{0,1},{3,2},{2,3},{5,4},{4,5},{7,6},{6,7},{9,8},{8,9},{11,10... | collective-permute-start | bytes 3538952 | tf_op jit(solution)/shard_map/ppermute | solution.py:19
  11.3 7.4 %copy-start.8 = (s32[2,8]{1,0:T(2,128)}, s32[2,8]{1,0:T(2,128)S(1)}, u32[]{:S(2)}) copy-start(s32[2,8]{1,0:T(2,128)S(1)} %get-tuple-element.25.refs_1_.refs_3_) | copy-start | bytes 196
  11.3 7.4 %copy-start.9 = (s32[2,8]{1,0:T(2,128)}, s32[2,8]{1,0:T(2,128)S(1)}, u32[]{:S(2)}) copy-start(s32[2,8]{1,0:T(2,128)S(1)} %get-tuple-element.24.refs_2_) | copy-start | bytes 196
  11.3 3.0 %collective-permute-start.7 = (s32[2,8]{1,0:T(2,128)S(1)}, s32[2,8]{1,0:T(2,128)S(1)}, u32[]{:S(2)}, u32[]{:S(2)}) collective-permute-start(s32[2,8]{1,0:T(2,128)S(1)} %get-tuple-element.24.refs_2_), channel_id=1, source_target_pairs={{6,0},{0,2},{2,4},{4,6},{7,1},{1,3},{3,5},{5,7},{14,8},{8,10},{10,... | collective-permute-start | bytes 200 | tf_op jit(solution)/shard_map/ppermute | solution.py:19
  11.4 5.4 %collective-permute-start.6 = (s32[2,8]{1,0:T(2,128)S(1)}, s32[2,8]{1,0:T(2,128)S(1)}, u32[]{:S(2)}, u32[]{:S(2)}) collective-permute-start(s32[2,8]{1,0:T(2,128)S(1)} %get-tuple-element.25.refs_1_.refs_3_), channel_id=1, source_target_pairs={{24,0},{0,8},{8,16},{16,24},{25,1},{1,9},{9,17},{17,25},{26,2},{2,... | collective-permute-start | bytes 200 | tf_op jit(solution)/shard_map/ppermute | solution.py:19
  13.0 65.4 %collective-permute-start.5 = (s32[2,32]{1,0:T(2,128)S(1)}, s32[2,32]{1,0:T(2,128)S(1)}, u32[]{:S(2)}, u32[]{:S(2)}) collective-permute-start(s32[2,32]{1,0:T(2,128)S(1)} %bitcast.35), channel_id=1, source_target_pairs={{1,0},{0,1},{3,2},{2,3},{5,4},{4,5},{7,6},{6,7},{9,8},{8,9},{11,10... | collective-permute-start | bytes 776 | tf_op jit(solution)/shard_map/ppermute | solution.py:19
  14.4 65.0 %copy-start.12 = (s32[2,8]{1,0:T(2,128)}, s32[2,8]{1,0:T(2,128)S(1)}, u32[]{:S(2)}) copy-start(s32[2,8]{1,0:T(2,128)S(1)} %collective-permute-done.7.refs_3_) | copy-start | bytes 196
  14.4 71.2 %collective-permute-start.2 = (f32[2,4,96,128]{3,2,0,1:T(8,128)S(1)}, f32[2,4,96,128]{3,2,0,1:T(8,128)S(1)}, u32[]{:S(2)}, u32[]{:S(2)}) collective-permute-start(f32[2,4,96,128]{3,2,0,1:T(8,128)S(1)} %get-tuple-element.18), channel_id=1, source_target_pairs={{24,0},{0,8},{8,16},{16,24},{25,1},{1,9},{9,17},{17,25},{26,2},{2,... | collective-permute-start | bytes 1179656 | tf_op jit(solution)/shard_map/ppermute | solution.py:19
  16.8 62.6 %copy-start.13 = (s32[2,8]{1,0:T(2,128)}, s32[2,8]{1,0:T(2,128)S(1)}, u32[]{:S(2)}) copy-start(s32[2,8]{1,0:T(2,128)S(1)} %collective-permute-done.6.refs_2_) | copy-start | bytes 196
  16.8 70.5 %collective-permute-start.1 = (f32[2,4,96,128]{3,2,0,1:T(8,128)S(1)}, f32[2,4,96,128]{3,2,0,1:T(8,128)S(1)}, u32[]{:S(2)}, u32[]{:S(2)}) collective-permute-start(f32[2,4,96,128]{3,2,0,1:T(8,128)S(1)} %get-tuple-element.19), channel_id=1, source_target_pairs={{8,0},{16,8},{24,16},{0,24},{9,1},{17,9},{25,17},{1,25},{10,2},{18... | collective-permute-start | bytes 1179656 | tf_op jit(solution)/shard_map/ppermute | solution.py:19
  18.7 72.5 %copy-start.1 = (f32[8,96,96]{2,1,0:T(8,128)}, f32[8,96,96]{2,1,0:T(8,128)S(1)}, u32[]{:S(2)}) copy-start(f32[8,96,96]{2,1,0:T(8,128)S(1)} %get-tuple-element.23.refs_5_) | copy-start | bytes 884740
  18.7 72.5 %copy-start.2 = (f32[8,96,96]{2,1,0:T(8,128)}, f32[8,96,96]{2,1,0:T(8,128)S(1)}, u32[]{:S(2)}) copy-start(f32[8,96,96]{2,1,0:T(8,128)S(1)} %get-tuple-element.22.refs_6_) | copy-start | bytes 884740
  78.4 12.8 %copy-start.14 = (s32[2,32]{1,0:T(2,128)}, s32[2,32]{1,0:T(2,128)S(1)}, u32[]{:S(2)}) copy-start(s32[2,32]{1,0:T(2,128)S(1)} %collective-permute-done.5.refs_1_) | copy-start | bytes 772
  78.4 7.2 %collective-permute-start.10 = (f32[8,96,96]{2,1,0:T(8,128)S(1)}, f32[8,96,96]{2,1,0:T(8,128)S(1)}, u32[]{:S(2)}, u32[]{:S(2)}) collective-permute-start(f32[8,96,96]{2,1,0:T(8,128)S(1)} %get-tuple-element.22.refs_6_), channel_id=1, source_target_pairs={{6,0},{0,2},{2,4},{4,6},{7,1},{1,3},{3,5},{5,7},{14,8},{8,10},{10,... | collective-permute-start | bytes 884744 | tf_op jit(solution)/shard_map/ppermute | solution.py:19
  85.6 1.8 copy-start.4
  85.6 57.4 %collective-permute-start.4 = (f32[2,4,96,128]{3,2,1,0:T(8,128)}, f32[2,4,96,128]{3,2,1,0:T(8,128)}, u32[]{:S(2)}, u32[]{:S(2)}) collective-permute-start(f32[2,4,96,128]{3,2,1,0:T(8,128)} %get-tuple-element.16), channel_id=1, source_target_pairs={{6,0},{0,2},{2,4},{4,6},{7,1},{1,3},{3,5},{5,7},{14,8},{8,10},{10,... | collective-permute-start | bytes 1179656 | tf_op jit(solution)/shard_map/ppermute | solution.py:19
  85.6 1.8 copy-start.5
  85.6 57.4 %collective-permute-start.3 = (f32[2,4,96,128]{3,2,1,0:T(8,128)}, f32[2,4,96,128]{3,2,1,0:T(8,128)}, u32[]{:S(2)}, u32[]{:S(2)}) collective-permute-start(f32[2,4,96,128]{3,2,1,0:T(8,128)} %get-tuple-element.17), channel_id=1, source_target_pairs={{2,0},{4,2},{6,4},{0,6},{3,1},{5,3},{7,5},{1,7},{10,8},{12,10},{14... | collective-permute-start | bytes 1179656 | tf_op jit(solution)/shard_map/ppermute | solution.py:19
  87.4 0.8 copy-start.7
  88.1 31.4 %collective-permute-start.9 = (f32[8,96,96]{2,1,0:T(8,128)S(1)}, f32[8,96,96]{2,1,0:T(8,128)}, u32[]{:S(2)}, u32[]{:S(2)}) collective-permute-start(f32[8,96,96]{2,1,0:T(8,128)S(1)} %get-tuple-element.23.refs_5_), channel_id=1, source_target_pairs={{24,0},{0,8},{8,16},{16,24},{25,1},{1,9},{9,17},{17,25},{26,2},{2,... | collective-permute-start | bytes 884744 | tf_op jit(solution)/shard_map/ppermute | solution.py:19
  91.2 25.7 %copy-start.6 = (f32[2,4,96,128]{3,2,0,1:T(8,128)S(1)}, f32[2,4,96,128]{3,2,0,1:T(8,128)}, u32[]{:S(2)}) copy-start(f32[2,4,96,128]{3,2,0,1:T(8,128)} %copy-done.5) | copy-start | bytes 1179652
where the time goes:
time: 248 us; the launch traced here: 247 us
  Pallas kernels  147 us (59%)
  waiting for transfers between devices  67.1 us (27%)
  starting transfers between devices  13.7 us (6%)
  local copies, waits for them, and re-layouts  11.6 us (5%)
  other arithmetic  7.31 us (3%)
    pallas_call x1, Pallas kernels, recur(): pl.pallas_call(functools.partial(recur_kernel, layers, nx, ny, normalizer...  100 us
    ppermute x11, waiting for transfers between devices, passed_along(): return lax.ppermute(block, axis, route)  67.1 us
    pallas_call x2, Pallas kernels, build(): pl.pallas_call(functools.partial(build_kernel, plan, edge), out_shape=[ja...  46.5 us
    ppermute x11, starting transfers between devices, passed_along(): return lax.ppermute(block, axis, route)  13.7 us
    mul x1, other arithmetic, shards(): initial = math.sqrt(2.0) * jnp.cos(phases[:, :, 0])  6.1 us
    ppermute x3, local copies, waits for them, and re-layouts, passed_along(): return lax.ppermute(block, axis, route)  5.26 us
  transfers between devices with their start and end apart: 11, of which 4 were waited for; matrix products, arithmetic and copies ran while one was open for 3% of the time, Pallas kernels for 19%

commit v1 on v0

--- a/solution.py
+++ b/solution.py
@@ -9,6 +9,7 @@
 from jax.sharding import PartitionSpec as P
 
 CHUNKS = 2
+TOGETHER = 4
 MESH = pl.DeviceIdType.MESH
 VMEM_LIMIT = 60 * 1024 * 1024
 
@@ -22,6 +23,17 @@
 def halves(values):
     high = values.astype(jnp.bfloat16)
     return high, (values - high.astype(jnp.float32)).astype(jnp.bfloat16)
+
+
+def packed(tiles):
+    count, degrees, _ = tiles.shape
+    spare = -degrees % 128
+    if spare == 0 or degrees % spare or count * spare % (128 * TOGETHER) or degrees % 8:
+        return tiles
+    pieces = degrees // spare
+    kept = count * degrees // 128
+    last = tiles[kept:].reshape(count - kept, degrees, pieces, spare).transpose(0, 2, 1, 3)
+    return jnp.concatenate([tiles[:kept], last.reshape(kept, degrees, spare)], axis=2)
 
 
 def build_kernel(plan, edge, *refs):
@@ -29,16 +41,25 @@
     pairs, tiles = refs[:n_src], refs[n_src : 2 * n_src]
     outs = refs[2 * n_src : 2 * n_src + len(plan)]
     block, wide, turn = refs[2 * n_src + len(plan) :]
-    degrees, slab = wide.shape
+    _, degrees, slab = wide.shape
     wide[...] = jnp.zeros_like(wide)
     turn[...] = jnp.zeros_like(turn)
 
-    def place(row, column, span, values):
-        wide[:, 0 : values.shape[1]] = values
-        group, slot = column // edge, column % edge
-        moved = pltpu.roll(wide[...], slot * degrees, 1)
-        start = pl.multiple_of(group * slab, slab)
-        block[row, :, pl.ds(start, slab)] += moved
+    def place(places):
+        for j, (_, _, values) in enumerate(places):
+            wide[j, :, 0 : values.shape[1]] = values
+        moved = [
+            pltpu.roll(wide[j], (column % edge) * degrees, 1)
+            for j, (_, column, _) in enumerate(places)
+        ]
+        for (row, column, _), values in zip(places, moved):
+            start = pl.multiple_of((column // edge) * slab, slab)
+            block[row, :, pl.ds(start, slab)] += values
+
+    def turned(j, tile):
+        for at, piece in tile:
+            turn[j, 0:degrees, at : at + piece.shape[1]] = piece
+        return turn[j].T[0:degrees]
 
     for out, (clusters, parts) in zip(outs, plan):
         span = clusters * degrees
@@ -49,21 +70,37 @@
 
         lax.fori_loop(0, clusters, clear, 0)
         for source, kind in parts:
-
-            def one(k, carry, source=source, kind=kind):
-                if kind == "diagonal":
-                    first, second = k, k
-                else:
-                    first, second = pairs[source][0, k], pairs[source][1, k]
-                tile = tiles[source][k]
-                if kind != "reverse":
-                    place(first, second, span, tile)
-                if kind != "forward":
-                    turn[0:degrees, 0:degrees] = tile
-                    place(second, first, span, turn[...].T[0:degrees])
+            stored = tiles[source]
+            spare = stored.shape[2] - degrees
+
+            def some(step, carry, source=source, kind=kind, stored=stored, first_tile=0, tail=False):
+                places = []
+                for j in range(TOGETHER):
+                    k = step * TOGETHER + j
+                    index = first_tile + k
+                    if kind == "diagonal":
+                        owner, partner = k, k
+                    else:
+                        owner, partner = pairs[source][0, index], pairs[source][1, index]
+                    if tail:
+                        pieces = degrees // spare
+                        tile = [
+                            (i * spare, stored[k * pieces + i][:, degrees:]) for i in range(pieces)
+                        ]
+                    else:
+                        tile = [(0, stored[k][:, 0:degrees])]
+                    if kind != "reverse":
+                        places.append((owner, partner, tile[0][1]))
+                    if kind != "forward":
+                        places.append((partner, owner, turned(j, tile)))
+                place(places)
                 return carry
 
-            lax.fori_loop(0, tiles[source].shape[0], one, 0)
+            count = stored.shape[0]
+            lax.fori_loop(0, count // TOGETHER, some, 0)
+            if spare:
+                rest = functools.partial(some, first_tile=count, tail=True)
+                lax.fori_loop(0, count * spare // degrees // TOGETHER, rest, 0)
 
         def write(i, carry, out=out, span=span):
             high, low = halves(block[i, :, 0:span])
@@ -75,8 +112,8 @@
         lax.fori_loop(0, clusters, write, 0)
 
 
-def build(plan, edge, pairs, tiles):
-    degrees = tiles[0].shape[-1]
+def build(plan, edge, pairs, tiles, cost):
+    degrees = tiles[0].shape[1]
     slab = edge * degrees
     most = max(clusters for clusters, _ in plan)
     around = -(-degrees // 128) * 128
@@ -90,11 +127,11 @@
         out_specs=[pl.BlockSpec(memory_space=pltpu.VMEM)] * len(plan),
         scratch_shapes=[
             pltpu.VMEM((most, degrees, most * degrees), jnp.float32),
-            pltpu.VMEM((degrees, slab), jnp.float32),
-            pltpu.VMEM((around, around), jnp.float32),
+            pltpu.VMEM((2 * TOGETHER, degrees, slab), jnp.float32),
+            pltpu.VMEM((TOGETHER, around, around), jnp.float32),
         ],
         compiler_params=pltpu.CompilerParams(vmem_limit_bytes=VMEM_LIMIT),
-        cost_estimate=pl.CostEstimate(flops=10**7, bytes_accessed=10**7, transcendentals=0),
+        cost_estimate=pl.CostEstimate(flops=250 * cost, bytes_accessed=cost, transcendentals=0),
     )(*pairs, *tiles)
 
 
@@ -102,8 +139,10 @@
     ways = min(layers - 1, 2)
     field0, first_layer = refs[0], refs[1 : 1 + ways]
     first_faces, refs = refs[1 + ways : 5 + ways], refs[5 + ways :]
-    own, across, sides, refs = refs[0], refs[1 : 1 + ways], refs[1 + ways : 5 + ways], refs[5 + ways :]
+    stored, refs = refs[: 5 + ways], refs[5 + ways :]
     out, moments, field1, field2, field3, got_layer, got_face, refs = *refs[:7], refs[7:]
+    loaded, load_sem, refs = refs[: 5 + ways], refs[5 + ways], refs[6 + ways :]
+    own, across, sides = loaded[0], loaded[1 : 1 + ways], loaded[1 + ways :]
     split, split_side, partial, got_y, got_x, send_sem, recv_sem, sum_send, sum_recv = refs
     chunks, edge, _, degrees, width = field0.shape
     slab = edge * degrees
@@ -115,13 +154,19 @@
     above = {"gz": lax.rem(me_z + 1, layers)}
     z_peers = [below, above][:ways]
 
+    loads = [
+        pltpu.make_async_copy(source, target, load_sem.at[j])
+        for j, (source, target) in enumerate(zip(stored, loaded))
+    ]
+    for load in loads:
+        load.start()
     barrier = pltpu.get_barrier_semaphore()
     for peer in x_peers + y_peers + z_peers:
         pl.semaphore_signal(barrier, inc=1, device_id=peer, device_id_type=MESH)
     pl.semaphore_wait(barrier, len(x_peers) + len(y_peers) + ways)
 
     def copies(op, ch):
-        field = fields[op + 1]
+        field = fields[op]
         found = []
         for j in range(ways):
             found.append((field.at[ch], got_layer.at[op, j, ch], z_peers[j]))
@@ -185,23 +230,30 @@
 
         return lax.fori_loop(0, edge, add, jnp.zeros((1, width), jnp.float32))
 
+    for ch in range(1, chunks):
+        for copy in copies(0, ch):
+            copy.start()
     partial[...] = jnp.zeros_like(partial)
     for op in range(3):
         field, target = fields[op], fields[op + 1]
 
         def step(ch, carry, op=op, field=field, target=target):
+            first = op == 0 and isinstance(ch, int) and ch == 0
+            if first:
+                loads[0].wait()
             apply(own, lambda i: field[ch, i], target, ch, True)
-            if op > 0:
-                for copy in copies(op - 1, ch):
+            if first:
+                for load in loads[1:]:
+                    load.wait()
+            else:
+                for copy in copies(op, ch):
                     copy.wait_recv()
             for j in range(ways):
-                if op == 0:
-                    apply(across[j], lambda i: first_layer[j][ch, i], target, ch, False)
+                if first:
+                    apply(across[j], lambda i: first_layer[j][i], target, ch, False)
                 else:
-                    apply(across[j], lambda i: got_layer[op - 1, j, ch, i], target, ch, False)
-            face = [
-                first_faces[j][ch] if op == 0 else got_face[op - 1, j, ch] for j in range(4)
-            ]
+                    apply(across[j], lambda i: got_layer[op, j, ch, i], target, ch, False)
+            face = [first_faces[j][...] if first else got_face[op, j, ch] for j in range(4)]
             target[ch, edge - 1] += side(0, face[0])
             target[ch, 0] += side(1, face[1])
             target[ch, :, edge - 1] += side(2, face[2])
@@ -214,7 +266,7 @@
 
                 lax.fori_loop(0, edge, combine, 0)
             if op < 2:
-                for copy in copies(op, ch):
+                for copy in copies(op + 1, ch):
                     copy.start()
             if op == 0:
                 partial[ch, 0:1] = inner(field, field, ch)
@@ -222,7 +274,11 @@
             partial[ch, 2 * op + 2 : 2 * op + 3] = inner(target, target, ch)
             return carry
 
-        lax.fori_loop(0, chunks, step, 0)
+        if op == 0:
+            for ch in range(chunks):
+                step(ch, 0)
+        else:
+            lax.fori_loop(0, chunks, step, 0)
 
     def gather(stage, peers, slots):
         sends = [
@@ -264,14 +320,14 @@
                 row = 2.0 * row - total[ch, k % 2 : k % 2 + 1]
             moments[0, k : k + 1, at] = row
 
-    for op in range(2):
+    for op in range(3):
 
         def finish(ch, carry, op=op):
             for copy in copies(op, ch):
                 copy.wait_send()
             return carry
 
-        lax.fori_loop(0, chunks, finish, 0)
+        lax.fori_loop(1 if op == 0 else 0, chunks, finish, 0)
 
 
 def recur(field, layer_fields, face_fields, own, across, sides, out_shape, normalizer):
@@ -287,21 +343,24 @@
             jax.ShapeDtypeStruct(out_shape, f32),
             jax.ShapeDtypeStruct((1, 7, chunks * width), f32),
         ],
-        in_specs=[pl.BlockSpec(memory_space=pltpu.VMEM)] * len(operands),
+        in_specs=[pl.BlockSpec(memory_space=pltpu.VMEM)] * (5 + ways)
+        + [pl.BlockSpec(memory_space=pl.ANY)] * (5 + ways),
         out_specs=[pl.BlockSpec(memory_space=pltpu.VMEM)] * 2,
         scratch_shapes=[
             pltpu.VMEM(field.shape, f32),
             pltpu.VMEM(field.shape, f32),
             pltpu.VMEM(field.shape, f32),
-            pltpu.VMEM((2, ways) + field.shape, f32),
-            pltpu.VMEM((2, 4, chunks, edge, degrees, width), f32),
+            pltpu.VMEM((3, ways) + field.shape, f32),
+            pltpu.VMEM((3, 4, chunks, edge, degrees, width), f32),
+            *[pltpu.VMEM(matrix.shape, matrix.dtype) for matrix in (own, *across, *sides)],
+            pltpu.SemaphoreType.DMA((5 + ways,)),
             pltpu.VMEM((rows, 2 * width), jnp.bfloat16),
             pltpu.VMEM((edge * degrees, 2 * width), jnp.bfloat16),
             pltpu.VMEM((chunks, 8, width), f32),
             pltpu.VMEM((ny - 1, chunks, 8, width), f32),
             pltpu.VMEM((nx - 1, chunks, 8, width), f32),
-            pltpu.SemaphoreType.DMA((2, chunks, ways + 4)),
-            pltpu.SemaphoreType.DMA((2, chunks, ways + 4)),
+            pltpu.SemaphoreType.DMA((3, chunks, ways + 4)),
+            pltpu.SemaphoreType.DMA((3, chunks, ways + 4)),
             pltpu.SemaphoreType.DMA((2, max(nx, ny) - 1)),
             pltpu.SemaphoreType.DMA((2, max(nx, ny) - 1)),
         ],
@@ -322,7 +381,7 @@
 
     own_layer, own_layer_pairs = layer_tiles[0, 0, 0], layer_pairs[0, 0, 0]
     faces, face_places = face_tiles[0, 0, 0], face_pairs[0, 0, 0]
-    below_set = passed_along(own_layer, "gz", 1)
+    below_set = passed_along(packed(own_layer), "gz", 1)
     below_pairs = passed_along(own_layer_pairs, "gz", 1)
     west_set = passed_along(faces[0], "gx", 1)
     west_pairs = passed_along(face_places[0], "gx", 1)
@@ -331,14 +390,14 @@
 
     initial = math.sqrt(2.0) * jnp.cos(phases[:, :, 0])
     field = jnp.stack([initial[..., i * width : (i + 1) * width] for i in range(CHUNKS)])
-    layer_fields = [passed_along(field, "gz", -1)]
+    layer_fields = [passed_along(field[0], "gz", -1)]
     if layers > 2:
-        layer_fields.append(passed_along(field, "gz", 1))
+        layer_fields.append(passed_along(field[0], "gz", 1))
     face_fields = [
-        passed_along(field[:, 0], "gx", -1),
-        passed_along(field[:, edge - 1], "gx", 1),
-        passed_along(field[:, :, 0], "gy", -1),
-        passed_along(field[:, :, edge - 1], "gy", 1),
+        passed_along(field[0, 0], "gx", -1),
+        passed_along(field[0, edge - 1], "gx", 1),
+        passed_along(field[0, :, 0], "gy", -1),
+        passed_along(field[0, :, edge - 1], "gy", 1),
     ]
 
     diagonal = diag_tiles.reshape(clusters, degrees, degrees)
@@ -351,6 +410,7 @@
         edge,
         [local_pairs[0, 0, 0], face_places[0], face_places[1], face_places[0]],
         [local_tiles[0, 0, 0], faces[0], faces[1], diagonal],
+        6 * 10**7,
     )
     if layers > 2:
         layer_plan = [(clusters, [(0, "forward")]), (clusters, [(1, "reverse")])]
@@ -361,6 +421,7 @@
         edge,
         [own_layer_pairs, below_pairs, west_pairs, south_pairs],
         [own_layer, below_set, west_set, south_set],
+        3 * 10**7,
     )
     normalizer = lax.axis_size("gx") * lax.axis_size("gy") * clusters * degrees
     order_three, moments = recur(

time: 248 us -> 188 us (0.76)
  waiting for transfers between devices: 67.1 us -> 17.9 us
  Pallas kernels: 147 us -> 135 us
    ppermute x11, waiting for transfers between devices: 67.1 us -> 17.9 us  [passed_along(): return lax.ppermute(block, axis, route)]
    pallas_call x2, Pallas kernels: 46.5 us -> 32.1 us  [build(): pl.pallas_call(functools.partial(build_kernel, plan, edge), out_shape=[ja...]
    ppermute x3 -> x1, local copies, waits for them, and re-layouts: 5.26 us -> 0.94 us  [passed_along(): return lax.ppermute(block, axis, route)]
  transfers between devices with their start and end apart: 11 -> 11, of which waited for: 4 -> 2; matrix products, arithmetic and copies ran while one was open for 3% -> 7% of each run, Pallas kernels for 19% -> 17%
where the time goes in v1:
time: 188 us; the launch traced here: 187 us
  Pallas kernels  135 us (72%)
  waiting for transfers between devices  17.9 us (10%)
  starting transfers between devices  15.4 us (8%)
  local copies, waits for them, and re-layouts  13.1 us (7%)
  other arithmetic  5.49 us (3%)
    pallas_call x1, Pallas kernels, recur(): pl.pallas_call(functools.partial(recur_kernel, layers, nx, ny, normalizer...  102 us
    pallas_call x2, Pallas kernels, build(): pl.pallas_call(functools.partial(build_kernel, plan, edge), out_shape=[ja...  32.1 us
    ppermute x11, waiting for transfers between devices, passed_along(): return lax.ppermute(block, axis, route)  17.9 us
    ppermute x11, starting transfers between devices, passed_along(): return lax.ppermute(block, axis, route)  15.4 us
    mul x1, other arithmetic, shards(): initial = math.sqrt(2.0) * jnp.cos(phases[:, :, 0])  4.97 us
  transfers between devices with their start and end apart: 11, of which 2 were waited for; matrix products, arithmetic and copies ran while one was open for 7% of the time, Pallas kernels for 17%

profile of v1, /device:TPU:0, one launch (start us, length us, event | category | flops | bytes accessed | tf_op | source)
XLA Modules:
  0.0 187.4 jit_solution(976205571731449617)
XLA Ops:
  0.6 0.0 copy-start.1
  0.6 1.4 slice_bitcast_fusion.8
  2.0 0.5 collective-permute-start.7
  2.5 2.1 %slice_bitcast_fusion.2 = (f32[8,96,96]{2,1,0:T(8,128)}, f32[8,96,96]{2,1,0:T(8,128)}) fusion(f32[1,1,1,2,8,96,96]{6,5,4,3,2,1,0:T(8,128)} %param.12), kind=kLoop, calls=%fused_computation.7 | loop fusion | bytes 1179648 | tf_op jit(solution)/shard_map/squeeze | solution.py:412
  4.5 2.6 %collective-permute-start.10 = (f32[8,96,96]{2,1,0:T(8,128)}, f32[8,96,96]{2,1,0:T(8,128)}, u32[]{:S(2)}, u32[]{:S(2)}) collective-permute-start(f32[8,96,96]{2,1,0:T(8,128)} %get-tuple-element.21.refs_6_), channel_id=1, source_target_pairs={{6,0},{0,2},{2,4},{4,6},{7,1},{1,3},{3,5},{5,7},{14,8},{8,10},{10,... | collective-permute-start | bytes 884744 | tf_op jit(solution)/shard_map/ppermute | solution.py:20
  7.1 1.6 collective-permute-start.9
  8.7 0.1 slice_bitcast_fusion
  8.8 0.2 copy.21
  9.0 0.4 copy.17
  9.4 0.0 copy-start
  9.4 0.4 pad_maximum_fusion.1
  9.8 1.6 collective-permute-start.8
  11.4 5.0 %fusion.1 = f32[4,4,96,256]{3,2,0,1:T(8,128)S(1)} fusion(f32[4,4,1,96,256]{4,3,2,1,0:T(8,128)S(1)} %copy-done), kind=kLoop, calls=%fused_computation.3 | loop fusion | flops 393216 | bytes 3145728 | tf_op jit(solution)/shard_map/mul | solution.py:391
  16.3 1.2 fusion.2
  17.5 1.0 collective-permute-start
  18.5 17.4 %shard_map.95 = (bf16[4,768,1536]{2,1,0:T(8,128)(2,1)}, bf16[1,768,384]{2,1,0:T(8,128)(2,1)}, bf16[1,768,384]{2,1,0:T(8,128)(2,1)}) custom-call(s32[2,48]{1,0:T(2,128)} %bitcast.38, s32[2,8]{1,0:T(2,128)} %get-tuple-element.28.refs_1_.refs_3_, s32[2,8]{1,0:T(2,128)} %copy-done.7, s32[2,8]{1,0:T(2,128)} %get-tuple-element.28.refs_1_.refs_3_, ...), custom_call_target="tpu_custom_call" | custom-call | flops 15000000512 | bytes 60000000 | tf_op jit(solution)/shard_map/pallas_call | solution.py:120
  35.9 0.7 slice_bitcast_fusion.6
  36.6 0.2 pad_maximum_fusion
  36.8 0.0 copy-start.8
  36.8 0.0 copy-start.6
  36.8 1.3 copy.18.refs_0_
  38.1 0.0 collective-permute-done.7.refs_3_
  38.1 1.1 collective-permute-start.5
  39.2 15.1 %collective-permute-done = f32[4,4,96,128]{3,2,0,1:T(8,128)S(1)} collective-permute-done((f32[4,4,96,128]{3,2,0,1:T(8,128)}, f32[4,4,96,128]{3,2,0,1:T(8,128)S(1)}, u32[]{:S(2)}, u32[]{:S(2)}) %collective-permute-start) | collective-permute-done | bytes 786464 | tf_op jit(solution)/shard_map/ppermute | solution.py:20
  54.3 1.6 collective-permute-start.6
  55.9 0.9 copy.19.refs_1_
  56.8 2.8 %collective-permute-done.6.refs_2_ = s32[2,8]{1,0:T(2,128)S(1)} collective-permute-done((s32[2,8]{1,0:T(2,128)S(1)}, s32[2,8]{1,0:T(2,128)S(1)}, u32[]{:S(2)}, u32[]{:S(2)}) %collective-permute-start.6) | collective-permute-done | bytes 96 | tf_op jit(solution)/shard_map/ppermute | solution.py:20
  59.7 0.0 collective-permute-start.2
  59.7 0.0 collective-permute-done.5.refs_1_
  59.7 0.0 copy-start.10
  59.7 3.8 %collective-permute-start.1 = (f32[4,96,128]{2,1,0:T(8,128)S(1)}, f32[4,96,128]{2,1,0:T(8,128)S(1)}, u32[]{:S(2)}, u32[]{:S(2)}) collective-permute-start(f32[4,96,128]{2,1,0:T(8,128)S(1)} %get-tuple-element.26), channel_id=1, source_target_pairs={{8,0},{16,8},{24,16},{0,24},{9,1},{17,9},{25,17},{1,25},{10,2},{18... | collective-permute-start | bytes 589832 | tf_op jit(solution)/shard_map/ppermute | solution.py:20
  63.5 0.0 collective-permute-done.10.refs_7_
  63.5 0.0 collective-permute-start.4
  63.5 0.0 collective-permute-done.9.refs_6_
  63.5 1.7 collective-permute-start.3
  65.3 0.0 collective-permute-done.8.refs_5_
  65.3 14.7 %shard_map.96 = (bf16[4,768,1536]{2,1,0:T(8,128)(2,1)}, bf16[1,768,384]{2,1,0:T(8,128)(2,1)}, bf16[1,768,384]{2,1,0:T(8,128)(2,1)}) custom-call(s32[2,32]{1,0:T(2,128)} %bitcast.39, s32[2,32]{1,0:T(2,128)} %copy-done.10, s32[2,8]{1,0:T(2,128)} %copy-done.11, s32[2,8]{1,0:T(2,128)} %copy-done.9, f32[32,96,96]{2,1,0:T(8,128)} %bitcast.34, ...), custom_call_target="tpu_custom_call" | custom-call | flops 7500000256 | bytes 30000000 | tf_op jit(solution)/shard_map/pallas_call | solution.py:120
  80.0 0.0 collective-permute-done.2.refs_3_
  80.0 0.0 collective-permute-done.1.refs_2_
  80.0 0.0 collective-permute-done.4.refs_5_
  80.1 0.0 collective-permute-done.3.refs_4_
  80.1 0.6 copy-done.2
  80.7 0.1 copy-done.3
  80.8 0.1 copy-done.4
  80.8 0.1 copy-done.5
  80.9 102.5 %shard_map.97 = (f32[4,4,1,96,256]{4,3,2,1,0:T(8,128)}, f32[1,7,256]{2,1,0:T(8,128)}) custom-call(f32[2,4,4,96,128]{4,3,2,1,0:T(8,128)} %copy.18.refs_0_, f32[4,4,96,128]{3,2,1,0:T(8,128)} %copy.19.refs_1_, f32[4,96,128]{2,1,0:T(8,128)} %copy-done.3, f32[4,96,128]{2,1,0:T(8,128)} %copy-done.2, f32[4,96,128]{2,1,0:T(8,128)} %copy-done.5, ...), custom_call_target="tpu_custom_call" | custom-call | tf_op jit(solution)/shard_map/pallas_call | solution.py:340
  183.4 1.3 copy.20
  184.7 2.7 %copy.28 = f32[4,4,1,96,256]{4,3,2,1,0:T(8,128)} copy(f32[4,4,1,96,256]{4,3,2,1,0:T(8,128)} %get-tuple-element.31) | data formatting | bytes 3145728
  (18 shorter events, 0.1 us)
Async XLA Ops:
  0.6 8.1 %copy-start.1 = (f32[1,1,1,32,96,96]{5,4,3,2,1,0:T(8,128)S(1)}, f32[1,1,1,32,96,96]{5,4,3,2,1,0:T(8,128)}, u32[]{:S(2)}) copy-start(f32[1,1,1,32,96,96]{5,4,3,2,1,0:T(8,128)} %param.14) | copy-start | bytes 3538948
  2.0 6.8 %copy-start.7 = (s32[2,8]{1,0:T(2,128)}, s32[2,8]{1,0:T(2,128)S(1)}, u32[]{:S(2)}) copy-start(s32[2,8]{1,0:T(2,128)S(1)} %get-tuple-element.27.refs_2_) | copy-start | bytes 196
  2.0 36.1 %collective-permute-start.7 = (s32[2,8]{1,0:T(2,128)S(1)}, s32[2,8]{1,0:T(2,128)S(1)}, u32[]{:S(2)}, u32[]{:S(2)}) collective-permute-start(s32[2,8]{1,0:T(2,128)S(1)} %get-tuple-element.27.refs_2_), channel_id=1, source_target_pairs={{6,0},{0,2},{2,4},{4,6},{7,1},{1,3},{3,5},{5,7},{14,8},{8,10},{10,... | collective-permute-start | bytes 200 | tf_op jit(solution)/shard_map/ppermute | solution.py:20
  4.5 59.0 %collective-permute-start.10 = (f32[8,96,96]{2,1,0:T(8,128)}, f32[8,96,96]{2,1,0:T(8,128)}, u32[]{:S(2)}, u32[]{:S(2)}) collective-permute-start(f32[8,96,96]{2,1,0:T(8,128)} %get-tuple-element.21.refs_6_), channel_id=1, source_target_pairs={{6,0},{0,2},{2,4},{4,6},{7,1},{1,3},{3,5},{5,7},{14,8},{8,10},{10,... | collective-permute-start | bytes 884744 | tf_op jit(solution)/shard_map/ppermute | solution.py:20
  7.1 1.7 slice-start
  7.1 56.4 %collective-permute-start.9 = (f32[8,96,96]{2,1,0:T(8,128)}, f32[8,96,96]{2,1,0:T(8,128)}, u32[]{:S(2)}, u32[]{:S(2)}) collective-permute-start(f32[8,96,96]{2,1,0:T(8,128)} %get-tuple-element.22.refs_5_), channel_id=1, source_target_pairs={{24,0},{0,8},{8,16},{16,24},{25,1},{1,9},{9,17},{17,25},{26,2},{2,... | collective-permute-start | bytes 884744 | tf_op jit(solution)/shard_map/ppermute | solution.py:20
  9.4 2.0 %copy-start = (f32[4,4,1,96,256]{4,3,2,1,0:T(8,128)S(1)}, f32[4,4,1,96,256]{4,3,2,1,0:T(8,128)}, u32[]{:S(2)}) copy-start(f32[4,4,1,96,256]{4,3,2,1,0:T(8,128)} %param.8) | copy-start | bytes 4718596
  9.8 55.5 %collective-permute-start.8 = (f32[24,96,128]{2,1,0:T(8,128)S(1)}, f32[24,96,128]{2,1,0:T(8,128)}, u32[]{:S(2)}, u32[]{:S(2)}) collective-permute-start(f32[24,96,128]{2,1,0:T(8,128)S(1)} %pad_maximum_fusion.1), channel_id=1, source_target_pairs={{1,0},{0,1},{3,2},{2,3},{5,4},{4,5},{7,6},{6,7},{9,8},{8,9},{11,10... | collective-permute-start | bytes 3538952 | tf_op jit(solution)/shard_map/ppermute | solution.py:20
  17.5 36.8 %collective-permute-start = (f32[4,4,96,128]{3,2,0,1:T(8,128)}, f32[4,4,96,128]{3,2,0,1:T(8,128)S(1)}, u32[]{:S(2)}, u32[]{:S(2)}) collective-permute-start(f32[4,4,96,128]{3,2,0,1:T(8,128)} %get-tuple-element.18), channel_id=1, source_target_pairs={{1,0},{0,1},{3,2},{2,3},{5,4},{4,5},{7,6},{6,7},{9,8},{8,9},{11,10... | collective-permute-start | bytes 2359304 | tf_op jit(solution)/shard_map/ppermute | solution.py:20
  36.8 1.3 copy-start.8
  36.8 17.5 %copy-start.6 = (s32[2,8]{1,0:T(2,128)S(1)}, s32[2,8]{1,0:T(2,128)}, u32[]{:S(2)}) copy-start(s32[2,8]{1,0:T(2,128)} %get-tuple-element.28.refs_1_.refs_3_) | copy-start | bytes 196
  38.1 27.2 %copy-start.9 = (s32[2,8]{1,0:T(2,128)}, s32[2,8]{1,0:T(2,128)S(1)}, u32[]{:S(2)}) copy-start(s32[2,8]{1,0:T(2,128)S(1)} %collective-permute-done.7.refs_3_) | copy-start | bytes 196
  38.1 21.6 %collective-permute-start.5 = (s32[2,32]{1,0:T(2,128)S(1)}, s32[2,32]{1,0:T(2,128)S(1)}, u32[]{:S(2)}, u32[]{:S(2)}) collective-permute-start(s32[2,32]{1,0:T(2,128)S(1)} %bitcast.40), channel_id=1, source_target_pairs={{1,0},{0,1},{3,2},{2,3},{5,4},{4,5},{7,6},{6,7},{9,8},{8,9},{11,10... | collective-permute-start | bytes 776 | tf_op jit(solution)/shard_map/ppermute | solution.py:20
  54.3 5.4 %collective-permute-start.6 = (s32[2,8]{1,0:T(2,128)S(1)}, s32[2,8]{1,0:T(2,128)S(1)}, u32[]{:S(2)}, u32[]{:S(2)}) collective-permute-start(s32[2,8]{1,0:T(2,128)S(1)} %copy-done.6), channel_id=1, source_target_pairs={{24,0},{0,8},{8,16},{16,24},{25,1},{1,9},{9,17},{17,25},{26,2},{2,... | collective-permute-start | bytes 200 | tf_op jit(solution)/shard_map/ppermute | solution.py:20
  59.7 5.6 %copy-start.11 = (s32[2,8]{1,0:T(2,128)}, s32[2,8]{1,0:T(2,128)S(1)}, u32[]{:S(2)}) copy-start(s32[2,8]{1,0:T(2,128)S(1)} %collective-permute-done.6.refs_2_) | copy-start | bytes 196
  59.7 20.3 %collective-permute-start.2 = (f32[4,96,128]{2,1,0:T(8,128)}, f32[4,96,128]{2,1,0:T(8,128)S(1)}, u32[]{:S(2)}, u32[]{:S(2)}) collective-permute-start(f32[4,96,128]{2,1,0:T(8,128)} %get-tuple-element.25), channel_id=1, source_target_pairs={{24,0},{0,8},{8,16},{16,24},{25,1},{1,9},{9,17},{17,25},{26,2},{2,... | collective-permute-start | bytes 589832 | tf_op jit(solution)/shard_map/ppermute | solution.py:20
  59.7 5.6 %copy-start.10 = (s32[2,32]{1,0:T(2,128)}, s32[2,32]{1,0:T(2,128)S(1)}, u32[]{:S(2)}) copy-start(s32[2,32]{1,0:T(2,128)S(1)} %collective-permute-done.5.refs_1_) | copy-start | bytes 772
  59.7 20.3 %collective-permute-start.1 = (f32[4,96,128]{2,1,0:T(8,128)S(1)}, f32[4,96,128]{2,1,0:T(8,128)S(1)}, u32[]{:S(2)}, u32[]{:S(2)}) collective-permute-start(f32[4,96,128]{2,1,0:T(8,128)S(1)} %get-tuple-element.26), channel_id=1, source_target_pairs={{8,0},{16,8},{24,16},{0,24},{9,1},{17,9},{25,17},{1,25},{10,2},{18... | collective-permute-start | bytes 589832 | tf_op jit(solution)/shard_map/ppermute | solution.py:20
  63.5 16.5 %collective-permute-start.4 = (f32[4,96,128]{2,1,0:T(8,128)S(1)}, f32[4,96,128]{2,1,0:T(8,128)S(1)}, u32[]{:S(2)}, u32[]{:S(2)}) collective-permute-start(f32[4,96,128]{2,1,0:T(8,128)S(1)} %get-tuple-element.23), channel_id=1, source_target_pairs={{6,0},{0,2},{2,4},{4,6},{7,1},{1,3},{3,5},{5,7},{14,8},{8,10},{10,... | collective-permute-start | bytes 589832 | tf_op jit(solution)/shard_map/ppermute | solution.py:20
  63.5 16.5 %collective-permute-start.3 = (f32[4,96,128]{2,1,0:T(8,128)S(1)}, f32[4,96,128]{2,1,0:T(8,128)S(1)}, u32[]{:S(2)}, u32[]{:S(2)}) collective-permute-start(f32[4,96,128]{2,1,0:T(8,128)S(1)} %get-tuple-element.24), channel_id=1, source_target_pairs={{2,0},{4,2},{6,4},{0,6},{3,1},{5,3},{7,5},{1,7},{10,8},{12,10},{14... | collective-permute-start | bytes 589832 | tf_op jit(solution)/shard_map/ppermute | solution.py:20
  80.0 0.7 copy-start.2
  80.0 0.7 copy-start.3
  80.0 0.8 copy-start.4
  80.1 0.8 copy-start.5

commit v2 on v1

--- a/solution.py
+++ b/solution.py
@@ -36,7 +36,18 @@
     return jnp.concatenate([tiles[:kept], last.reshape(kept, degrees, spare)], axis=2)
 
 
-def build_kernel(plan, edge, *refs):
+def with_pairs(tiles, pairs):
+    _, degrees, lanes = tiles.shape
+    spare = ((0, degrees - pairs.shape[0]), (0, lanes - pairs.shape[1]))
+    return jnp.concatenate([tiles, jnp.pad(pairs.astype(jnp.float32), spare)[None]])
+
+
+def sent_along(tiles, pairs, axis):
+    received = passed_along(with_pairs(tiles, pairs), axis, 1)
+    return received, received[-1, 0:2, 0 : pairs.shape[1]].astype(jnp.int32)
+
+
+def build_kernel(plan, counts, edge, *refs):
     n_src = 1 + max(source for _, parts in plan for source, _ in parts)
     pairs, tiles = refs[:n_src], refs[n_src : 2 * n_src]
     outs = refs[2 * n_src : 2 * n_src + len(plan)]
@@ -96,7 +107,7 @@
                 place(places)
                 return carry
 
-            count = stored.shape[0]
+            count = counts[source]
             lax.fori_loop(0, count // TOGETHER, some, 0)
             if spare:
                 rest = functools.partial(some, first_tile=count, tail=True)
@@ -112,13 +123,13 @@
         lax.fori_loop(0, clusters, write, 0)
 
 
-def build(plan, edge, pairs, tiles, cost):
+def build(plan, counts, edge, pairs, tiles, cost):
     degrees = tiles[0].shape[1]
     slab = edge * degrees
     most = max(clusters for clusters, _ in plan)
     around = -(-degrees // 128) * 128
     return pl.pallas_call(
-        functools.partial(build_kernel, plan, edge),
+        functools.partial(build_kernel, plan, counts, edge),
         out_shape=[
             jax.ShapeDtypeStruct((c // edge, 2 * slab, c * degrees), jnp.bfloat16) for c, _ in plan
         ],
@@ -138,7 +149,7 @@
 def recur_kernel(layers, width_x, width_y, normalizer, *refs):
     ways = min(layers - 1, 2)
     field0, first_layer = refs[0], refs[1 : 1 + ways]
-    first_faces, refs = refs[1 + ways : 5 + ways], refs[5 + ways :]
+    refs = refs[1 + ways :]
     stored, refs = refs[: 5 + ways], refs[5 + ways :]
     out, moments, field1, field2, field3, got_layer, got_face, refs = *refs[:7], refs[7:]
     loaded, load_sem, refs = refs[: 5 + ways], refs[5 + ways], refs[6 + ways :]
@@ -230,8 +241,8 @@
 
         return lax.fori_loop(0, edge, add, jnp.zeros((1, width), jnp.float32))
 
-    for ch in range(1, chunks):
-        for copy in copies(0, ch):
+    for ch in range(chunks):
+        for copy in copies(0, ch)[: 4 if ch == 0 else None]:
             copy.start()
     partial[...] = jnp.zeros_like(partial)
     for op in range(3):
@@ -253,7 +264,10 @@
                     apply(across[j], lambda i: first_layer[j][i], target, ch, False)
                 else:
                     apply(across[j], lambda i: got_layer[op, j, ch, i], target, ch, False)
-            face = [first_faces[j][...] if first else got_face[op, j, ch] for j in range(4)]
+            if first:
+                for copy in copies(0, 0)[:4]:
+                    copy.wait_recv()
+            face = [got_face[op, j, ch] for j in range(4)]
             target[ch, edge - 1] += side(0, face[0])
             target[ch, 0] += side(1, face[1])
             target[ch, :, edge - 1] += side(2, face[2])
@@ -318,8 +332,10 @@
             row = total[ch, k : k + 1]
             if k > 1:
                 row = 2.0 * row - total[ch, k % 2 : k % 2 + 1]
-            moments[0, k : k + 1, at] = row
-
+            moments[k, :, at] = row
+
+    for copy in copies(0, 0)[:4]:
+        copy.wait_send()
     for op in range(3):
 
         def finish(ch, carry, op=op):
@@ -330,20 +346,20 @@
         lax.fori_loop(1 if op == 0 else 0, chunks, finish, 0)
 
 
-def recur(field, layer_fields, face_fields, own, across, sides, out_shape, normalizer):
+def recur(field, layer_fields, own, across, sides, out_shape, normalizer):
     chunks, edge, _, degrees, width = field.shape
     layers, nx, ny = lax.axis_size("gz"), lax.axis_size("gx"), lax.axis_size("gy")
     ways = len(layer_fields)
-    operands = [field, *layer_fields, *face_fields, own, *across, *sides]
+    operands = [field, *layer_fields, own, *across, *sides]
     f32 = jnp.float32
     rows = edge * edge * degrees
     return pl.pallas_call(
         functools.partial(recur_kernel, layers, nx, ny, normalizer),
         out_shape=[
             jax.ShapeDtypeStruct(out_shape, f32),
-            jax.ShapeDtypeStruct((1, 7, chunks * width), f32),
+            jax.ShapeDtypeStruct((7, 1, chunks * width), f32),
         ],
-        in_specs=[pl.BlockSpec(memory_space=pltpu.VMEM)] * (5 + ways)
+        in_specs=[pl.BlockSpec(memory_space=pltpu.VMEM)] * (1 + ways)
         + [pl.BlockSpec(memory_space=pl.ANY)] * (5 + ways),
         out_specs=[pl.BlockSpec(memory_space=pltpu.VMEM)] * 2,
         scratch_shapes=[
@@ -381,25 +397,16 @@
 
     own_layer, own_layer_pairs = layer_tiles[0, 0, 0], layer_pairs[0, 0, 0]
     faces, face_places = face_tiles[0, 0, 0], face_pairs[0, 0, 0]
-    below_set = passed_along(packed(own_layer), "gz", 1)
-    below_pairs = passed_along(own_layer_pairs, "gz", 1)
-    west_set = passed_along(faces[0], "gx", 1)
-    west_pairs = passed_along(face_places[0], "gx", 1)
-    south_set = passed_along(faces[1], "gy", 1)
-    south_pairs = passed_along(face_places[1], "gy", 1)
+    layer_packed = packed(own_layer)
+    below_set, below_pairs = sent_along(layer_packed, own_layer_pairs, "gz")
+    west_set, west_pairs = sent_along(faces[0], face_places[0], "gx")
+    south_set, south_pairs = sent_along(faces[1], face_places[1], "gy")
 
     initial = math.sqrt(2.0) * jnp.cos(phases[:, :, 0])
     field = jnp.stack([initial[..., i * width : (i + 1) * width] for i in range(CHUNKS)])
     layer_fields = [passed_along(field[0], "gz", -1)]
     if layers > 2:
         layer_fields.append(passed_along(field[0], "gz", 1))
-    face_fields = [
-        passed_along(field[0, 0], "gx", -1),
-        passed_along(field[0, edge - 1], "gx", 1),
-        passed_along(field[0, :, 0], "gy", -1),
-        passed_along(field[0, :, edge - 1], "gy", 1),
-    ]
-
     diagonal = diag_tiles.reshape(clusters, degrees, degrees)
     own, east, north = build(
         [
@@ -407,6 +414,7 @@
             (edge, [(1, "forward")]),
             (edge, [(2, "forward")]),
         ],
+        [local_tiles.shape[3], faces.shape[1], faces.shape[1], clusters],
         edge,
         [local_pairs[0, 0, 0], face_places[0], face_places[1], face_places[0]],
         [local_tiles[0, 0, 0], faces[0], faces[1], diagonal],
@@ -418,6 +426,7 @@
         layer_plan = [(clusters, [(0, "forward"), (1, "reverse")])]
     *across, west, south = build(
         layer_plan + [(edge, [(2, "reverse")]), (edge, [(3, "reverse")])],
+        [own_layer.shape[0], layer_packed.shape[0], faces.shape[1], faces.shape[1]],
         edge,
         [own_layer_pairs, below_pairs, west_pairs, south_pairs],
         [own_layer, below_set, west_set, south_set],
@@ -427,14 +436,13 @@
     order_three, moments = recur(
         field,
         layer_fields,
-        face_fields,
         own,
         across,
         [east, west, north, south],
         (edge, edge, 1, degrees, columns),
         float(normalizer),
     )
-    return order_three, moments
+    return order_three, moments.transpose(1, 0, 2)
 
 
 def solution(mesh):

time: 188 us -> 165 us (0.88)
  waiting for transfers between devices: 17.9 us -> 2.04 us
  starting transfers between devices: 15.4 us -> 5.12 us
  other arithmetic: 5.49 us -> 14.4 us
  local copies, waits for them, and re-layouts: 13.1 us -> 7.19 us
    ppermute x11 -> x4, waiting for transfers between devices: 17.9 us -> 2.04 us  [passed_along(): return lax.ppermute(block, axis, route)]
    ppermute x11 -> x4, starting transfers between devices: 15.4 us -> 5.12 us  [passed_along(): return lax.ppermute(block, axis, route)]
    convert_element_type x0 -> x5, other arithmetic: none -> 5.03 us  [the longest x3 3.75 us: sent_along(): return (received, received[-1, 0:2, 0:pairs.shape[1]].astype(jnp.int32))]
    concatenate x1 -> x3, other arithmetic: 0.37 us -> 3.04 us  [with_pairs(): jnp.concatenate([tiles, jnp.pad(pairs.astype(jnp.float32), spare)[None]])]
    squeeze x3 -> x0, local copies, waits for them, and re-layouts: 2.1 us -> none  [the longest x1 1.38 us: shards(): face_places[1]]
    unnamed x26 -> x17, local copies, waits for them, and re-layouts: 3.72 us -> 4.94 us
  transfers between devices with their start and end apart: 11 -> 4, of which waited for: 2 -> 2; matrix products, arithmetic and copies ran while one was open for 7% -> 8% of each run, Pallas kernels for 17% -> 20%
where the time goes in v2:
time: 165 us
  Pallas kernels  135 us (82%)
  other arithmetic  14.4 us (9%)
  local copies, waits for them, and re-layouts  7.19 us (4%)
  starting transfers between devices  5.12 us (3%)
  waiting for transfers between devices  2.04 us (1%)
    pallas_call x1, Pallas kernels, recur(): pl.pallas_call(functools.partial(recur_kernel, layers, nx, ny, normalizer...  103 us
    pallas_call x2, Pallas kernels, build(): pl.pallas_call(functools.partial(build_kernel, plan, counts, edge), out_s...  32.2 us
    ppermute x4, starting transfers between devices, passed_along(): return lax.ppermute(block, axis, route)  5.12 us
    mul x1, other arithmetic, shards(): initial = math.sqrt(2.0) * jnp.cos(phases[:, :, 0])  5.07 us
    unnamed x17, local copies, waits for them, and re-layouts  4.94 us
    convert_element_type x3, other arithmetic, sent_along(): return (received, received[-1, 0:2, 0:pairs.shape[1]].astype(jnp.int32))  3.75 us
  transfers between devices with their start and end apart: 4, of which 2 were waited for; matrix products, arithmetic and copies ran while one was open for 8% of the time, Pallas kernels for 20%

profile of v2, /device:TPU:0, one launch (start us, length us, event | category | flops | bytes accessed | tf_op | source)
XLA Modules:
  0.0 164.8 jit_solution(8093977649078803444)
XLA Ops:
  0.6 1.3 fusion.6
  1.9 1.2 slice_bitcast_fusion.2
  3.1 0.0 copy-start.3
  3.1 0.0 copy-start.2
  3.1 0.0 copy-start.1
  3.1 0.8 pad_maximum_fusion.2
  3.9 3.0 %collective-permute-start.2 = (f32[9,96,96]{2,1,0:T(8,128)}, f32[9,96,96]{2,1,0:T(8,128)}, u32[]{:S(2)}, u32[]{:S(2)}) collective-permute-start(f32[9,96,96]{2,1,0:T(8,128)} %pad_maximum_fusion.2), channel_id=1, source_target_pairs={{24,0},{0,8},{8,16},{16,24},{25,1},{1,9},{9,17},{17,25},{26,2},{2,... | collective-permute-start | bytes 995336 | tf_op jit(solution)/shard_map/ppermute | solution.py:20
  7.0 0.0 copy-done.3
  7.0 0.8 pad_maximum_fusion.3
  7.8 0.0 copy-start.6
  7.8 0.0 slice-start
  7.8 0.0 collective-permute-start.3
  7.8 0.0 copy-done.1
  7.8 0.1 slice_bitcast_fusion
  7.9 0.0 copy-done.2
  7.9 0.6 copy-done.6
  8.5 0.3 slice-done
  8.8 0.2 copy.15
  8.9 0.4 copy.14
  9.3 0.0 copy-start
  9.3 1.4 pad_maximum_fusion.1
  10.8 1.5 collective-permute-start.1
  12.3 0.0 copy-done
  12.3 5.1 %fusion.1 = f32[4,4,96,256]{3,2,1,0:T(8,128)S(1)} fusion(f32[4,4,1,96,256]{4,3,2,1,0:T(8,128)S(1)} %copy-done), kind=kLoop, calls=%fused_computation.3 | loop fusion | flops 393216 | bytes 3145728 | tf_op jit(solution)/shard_map/mul | solution.py:405
  17.4 0.3 fusion.7
  17.7 0.6 collective-permute-start
  18.2 17.4 %shard_map.95 = (bf16[4,768,1536]{2,1,0:T(8,128)(2,1)}, bf16[1,768,384]{2,1,0:T(8,128)(2,1)}, bf16[1,768,384]{2,1,0:T(8,128)(2,1)}) custom-call(s32[2,48]{1,0:T(2,128)} %bitcast.56, s32[2,8]{1,0:T(2,128)} %get-tuple-element.26.refs_1_.refs_3_, s32[2,8]{1,0:T(2,128)} %get-tuple-element.25.refs_2_, s32[2,8]{1,0:T(2,128)} %get-tuple-element.26.refs_1_.refs_3_, ...), custom_call_target="tpu_custom_call" | custom-call | flops 15000000512 | bytes 60000000 | tf_op jit(solution)/shard_map/pallas_call | solution.py:131
  35.7 1.3 pad_maximum_fusion.refs_0_
  37.0 0.0 collective-permute-done.2.refs_6_
  37.0 1.3 fusion.3.refs_2_
  38.2 0.0 collective-permute-done.3.refs_7_
  38.2 1.2 fusion.2.refs_3_
  39.5 1.5 collective-permute-done.1.refs_5_
  41.0 1.2 fusion.4.refs_1_
  42.2 14.8 %shard_map.96 = (bf16[4,768,1536]{2,1,0:T(8,128)(2,1)}, bf16[1,768,384]{2,1,0:T(8,128)(2,1)}, bf16[1,768,384]{2,1,0:T(8,128)(2,1)}) custom-call(s32[2,32]{1,0:T(2,128)} %bitcast.53, s32[2,32]{1,0:T(2,128)} %fusion.4.refs_1_, s32[2,8]{1,0:T(2,128)} %fusion.3.refs_2_, s32[2,8]{1,0:T(2,128)} %fusion.2.refs_3_, f32[32,96,96]{2,1,0:T(8,128)} %bitcast.50, ...), custom_call_target="tpu_custom_call" | custom-call | flops 7500000256 | bytes 30000000 | tf_op jit(solution)/shard_map/pallas_call | solution.py:131
  57.0 0.5 collective-permute-done.refs_1_
  57.5 0.0 copy-start.4
  57.5 0.9 copy-done.4
  58.4 103.1 %shard_map.97 = (f32[4,4,1,96,256]{4,3,2,1,0:T(8,128)}, f32[7,1,256]{2,1,0:T(1,128)}) custom-call(f32[2,4,4,96,128]{4,3,2,1,0:T(8,128)} %pad_maximum_fusion.refs_0_, f32[4,4,96,128]{3,2,1,0:T(8,128)} %copy-done.4, bf16[4,768,1536]{2,1,0:T(8,128)(2,1)} %get-tuple-element.10.refs_2_, bf16[4,768,1536]{2,1,0:T(8,128)(2,1)} %get-tuple-element.11.refs_3_, ...), custom_call_target="tpu_custom_call" | custom-call | tf_op jit(solution)/shard_map/pallas_call | solution.py:356
  161.5 0.0 copy-start.5
  161.5 2.7 %copy.18 = f32[4,4,1,96,256]{4,3,2,1,0:T(8,128)} copy(f32[4,4,1,96,256]{4,3,2,1,0:T(8,128)} %get-tuple-element.29) | data formatting | bytes 3145728
  164.2 0.0 copy-done.5
  164.2 0.6 copy.19
  (4 shorter events, 0.0 us)
Async XLA Ops:
  3.1 3.9 %copy-start.3 = (f32[8,96,96]{2,1,0:T(8,128)}, f32[8,96,96]{2,1,0:T(8,128)S(1)}, u32[]{:S(2)}) copy-start(f32[8,96,96]{2,1,0:T(8,128)S(1)} %get-tuple-element.22.refs_5_) | copy-start | bytes 884740
  3.1 4.8 %copy-start.2 = (f32[8,96,96]{2,1,0:T(8,128)}, f32[8,96,96]{2,1,0:T(8,128)S(1)}, u32[]{:S(2)}) copy-start(f32[8,96,96]{2,1,0:T(8,128)S(1)} %get-tuple-element.21.refs_6_) | copy-start | bytes 884740
  3.1 4.7 %copy-start.1 = (f32[1,1,1,32,96,96]{5,4,3,2,1,0:T(8,128)S(1)}, f32[1,1,1,32,96,96]{5,4,3,2,1,0:T(8,128)}, u32[]{:S(2)}) copy-start(f32[1,1,1,32,96,96]{5,4,3,2,1,0:T(8,128)} %param.14) | copy-start | bytes 3538948
  3.9 33.0 %collective-permute-start.2 = (f32[9,96,96]{2,1,0:T(8,128)}, f32[9,96,96]{2,1,0:T(8,128)}, u32[]{:S(2)}, u32[]{:S(2)}) collective-permute-start(f32[9,96,96]{2,1,0:T(8,128)} %pad_maximum_fusion.2), channel_id=1, source_target_pairs={{24,0},{0,8},{8,16},{16,24},{25,1},{1,9},{9,17},{17,25},{26,2},{2,... | collective-permute-start | bytes 995336 | tf_op jit(solution)/shard_map/ppermute | solution.py:20
  7.8 0.7 copy-start.6
  7.8 1.0 slice-start
  7.8 30.5 %collective-permute-start.3 = (f32[9,96,96]{2,1,0:T(8,128)}, f32[9,96,96]{2,1,0:T(8,128)}, u32[]{:S(2)}, u32[]{:S(2)}) collective-permute-start(f32[9,96,96]{2,1,0:T(8,128)} %pad_maximum_fusion.3), channel_id=1, source_target_pairs={{6,0},{0,2},{2,4},{4,6},{7,1},{1,3},{3,5},{5,7},{14,8},{8,10},{10,... | collective-permute-start | bytes 995336 | tf_op jit(solution)/shard_map/ppermute | solution.py:20
  9.3 3.0 %copy-start = (f32[4,4,1,96,256]{4,3,2,1,0:T(8,128)S(1)}, f32[4,4,1,96,256]{4,3,2,1,0:T(8,128)}, u32[]{:S(2)}) copy-start(f32[4,4,1,96,256]{4,3,2,1,0:T(8,128)} %param.8) | copy-start | bytes 4718596
  10.8 30.2 %collective-permute-start.1 = (f32[25,96,128]{2,1,0:T(8,128)}, f32[25,96,128]{2,1,0:T(8,128)}, u32[]{:S(2)}, u32[]{:S(2)}) collective-permute-start(f32[25,96,128]{2,1,0:T(8,128)} %pad_maximum_fusion.1), channel_id=1, source_target_pairs={{1,0},{0,1},{3,2},{2,3},{5,4},{4,5},{7,6},{6,7},{9,8},{8,9},{11,10... | collective-permute-start | bytes 3686408 | tf_op jit(solution)/shard_map/ppermute | solution.py:20
  17.7 39.8 %collective-permute-start = (f32[4,4,96,128]{3,2,1,0:T(8,128)S(1)}, f32[4,4,96,128]{3,2,1,0:T(8,128)S(1)}, u32[]{:S(2)}, u32[]{:S(2)}) collective-permute-start(f32[4,4,96,128]{3,2,1,0:T(8,128)S(1)} %get-tuple-element.18), channel_id=1, source_target_pairs={{1,0},{0,1},{3,2},{2,3},{5,4},{4,5},{7,6},{6,7},{9,8},{8,9},{11,10... | collective-permute-start | bytes 2359304 | tf_op jit(solution)/shard_map/ppermute | solution.py:20
  57.5 0.9 copy-start.4
  161.5 2.7 %copy-start.5 = (f32[7,1,256]{2,1,0:T(1,128)S(1)}, f32[7,1,256]{2,1,0:T(1,128)}, u32[]{:S(2)}) copy-start(f32[7,1,256]{2,1,0:T(1,128)} %get-tuple-element.17) | copy-start | bytes 21508

commit v3 on v2

--- a/solution.py
+++ b/solution.py
@@ -10,6 +10,7 @@
 
 CHUNKS = 2
 TOGETHER = 4
+PIECES = 2
 MESH = pl.DeviceIdType.MESH
 VMEM_LIMIT = 60 * 1024 * 1024
 
@@ -42,8 +43,8 @@
     return jnp.concatenate([tiles, jnp.pad(pairs.astype(jnp.float32), spare)[None]])
 
 
-def sent_along(tiles, pairs, axis):
-    received = passed_along(with_pairs(tiles, pairs), axis, 1)
+def sent_along(carried, pairs, axis):
+    received = passed_along(carried, axis, 1)
     return received, received[-1, 0:2, 0 : pairs.shape[1]].astype(jnp.int32)
 
 
@@ -157,6 +158,7 @@
     split, split_side, partial, got_y, got_x, send_sem, recv_sem, sum_send, sum_recv = refs
     chunks, edge, _, degrees, width = field0.shape
     slab = edge * degrees
+    pieces = PIECES if edge % PIECES == 0 else 1
     fields = [field0, field1, field2, field3]
     me_x, me_y, me_z = lax.axis_index("gx"), lax.axis_index("gy"), lax.axis_index("gz")
     x_peers = [{"gx": lax.rem(me_x + d, width_x)} for d in range(1, width_x)]
@@ -180,7 +182,11 @@
         field = fields[op]
         found = []
         for j in range(ways):
-            found.append((field.at[ch], got_layer.at[op, j, ch], z_peers[j]))
+            for p in range(pieces):
+                piece = pl.ds(p * (edge // pieces), edge // pieces)
+                found.append(
+                    (field.at[ch, piece], got_layer.at[op, j, ch, piece], z_peers[j])
+                )
         ends = [
             (field.at[ch, 0], x_peers[-1]),
             (field.at[ch, edge - 1], x_peers[0]),
@@ -189,7 +195,7 @@
         ]
         for j, (source, peer) in enumerate(ends):
             found.append((source, got_face.at[op, j, ch], peer))
-        order = found[ways:] + found[:ways]
+        order = found[ways * pieces :] + found[: ways * pieces]
         return [
             pltpu.make_async_remote_copy(
                 src_ref=source,
@@ -211,15 +217,16 @@
         four = both[0:slab] + both[slab : 2 * slab]
         return four[:, 0:width] + four[:, width : 2 * width]
 
-    def apply(matrix, source, target, ch, fresh):
+    def apply(matrix, source, target, ch, fresh, begin, end):
         def fill(i, carry):
             into_split(source(i), i)
             return carry
 
-        lax.fori_loop(0, edge, fill, 0)
+        lax.fori_loop(begin, end, fill, 0)
+        rows = slice(begin * slab, end * slab)
 
         def part(i, carry):
-            both = jnp.dot(matrix[i], split[...], preferred_element_type=jnp.float32)
+            both = jnp.dot(matrix[i, :, rows], split[rows], preferred_element_type=jnp.float32)
             value = folded(both).reshape(edge, degrees, width)
             target[ch, i] = value if fresh else target[ch, i] + value
             return carry
@@ -252,26 +259,34 @@
             first = op == 0 and isinstance(ch, int) and ch == 0
             if first:
                 loads[0].wait()
-            apply(own, lambda i: field[ch, i], target, ch, True)
+            apply(own, lambda i: field[ch, i], target, ch, True, 0, edge)
             if first:
                 for load in loads[1:]:
                     load.wait()
-            else:
-                for copy in copies(op, ch):
-                    copy.wait_recv()
-            for j in range(ways):
-                if first:
-                    apply(across[j], lambda i: first_layer[j][i], target, ch, False)
-                else:
-                    apply(across[j], lambda i: got_layer[op, j, ch, i], target, ch, False)
-            if first:
-                for copy in copies(0, 0)[:4]:
-                    copy.wait_recv()
+            arrivals = copies(op, ch)
+            for copy in arrivals[:4]:
+                copy.wait_recv()
             face = [got_face[op, j, ch] for j in range(4)]
             target[ch, edge - 1] += side(0, face[0])
             target[ch, 0] += side(1, face[1])
             target[ch, :, edge - 1] += side(2, face[2])
             target[ch, :, 0] += side(3, face[3])
+            for j in range(ways):
+                for p in range(pieces):
+                    begin, end = p * (edge // pieces), (p + 1) * (edge // pieces)
+                    if first:
+                        apply(across[j], lambda i: first_layer[j][i], target, ch, False, begin, end)
+                    else:
+                        arrivals[4 + j * pieces + p].wait_recv()
+                        apply(
+                            across[j],
+                            lambda i: got_layer[op, j, ch, i],
+                            target,
+                            ch,
+                            False,
+                            begin,
+                            end,
+                        )
             if op > 0:
 
                 def combine(i, carry):
@@ -375,8 +390,8 @@
             pltpu.VMEM((chunks, 8, width), f32),
             pltpu.VMEM((ny - 1, chunks, 8, width), f32),
             pltpu.VMEM((nx - 1, chunks, 8, width), f32),
-            pltpu.SemaphoreType.DMA((3, chunks, ways + 4)),
-            pltpu.SemaphoreType.DMA((3, chunks, ways + 4)),
+            pltpu.SemaphoreType.DMA((3, chunks, PIECES * ways + 4)),
+            pltpu.SemaphoreType.DMA((3, chunks, PIECES * ways + 4)),
             pltpu.SemaphoreType.DMA((2, max(nx, ny) - 1)),
             pltpu.SemaphoreType.DMA((2, max(nx, ny) - 1)),
         ],
@@ -398,9 +413,10 @@
     own_layer, own_layer_pairs = layer_tiles[0, 0, 0], layer_pairs[0, 0, 0]
     faces, face_places = face_tiles[0, 0, 0], face_pairs[0, 0, 0]
     layer_packed = packed(own_layer)
-    below_set, below_pairs = sent_along(layer_packed, own_layer_pairs, "gz")
-    west_set, west_pairs = sent_along(faces[0], face_places[0], "gx")
-    south_set, south_pairs = sent_along(faces[1], face_places[1], "gy")
+    carried = with_pairs(layer_packed, own_layer_pairs)
+    below_set, below_pairs = sent_along(carried, own_layer_pairs, "gz")
+    west_set, west_pairs = sent_along(with_pairs(faces[0], face_places[0]), face_places[0], "gx")
+    south_set, south_pairs = sent_along(with_pairs(faces[1], face_places[1]), face_places[1], "gy")
 
     initial = math.sqrt(2.0) * jnp.cos(phases[:, :, 0])
     field = jnp.stack([initial[..., i * width : (i + 1) * width] for i in range(CHUNKS)])

time: 165 us -> 164 us (level)
  no operation moved by 1% of the time
where the time goes in v3:
time: 164 us; the launch traced here: 163 us
  Pallas kernels  134 us (82%)
  other arithmetic  14.4 us (9%)
  local copies, waits for them, and re-layouts  7.19 us (4%)
  starting transfers between devices  5.12 us (3%)
  waiting for transfers between devices  2.04 us (1%)
    pallas_call x1, Pallas kernels, recur(): pl.pallas_call(functools.partial(recur_kernel, layers, nx, ny, normalizer...  102 us
    pallas_call x2, Pallas kernels, build(): pl.pallas_call(functools.partial(build_kernel, plan, counts, edge), out_s...  32.2 us
    ppermute x4, starting transfers between devices, passed_along(): return lax.ppermute(block, axis, route)  5.12 us
    mul x1, other arithmetic, shards(): initial = math.sqrt(2.0) * jnp.cos(phases[:, :, 0])  5.07 us
    unnamed x17, local copies, waits for them, and re-layouts  4.94 us
    convert_element_type x3, other arithmetic, sent_along(): return (received, received[-1, 0:2, 0:pairs.shape[1]].astype(jnp.int32))  3.75 us
  transfers between devices with their start and end apart: 4, of which 2 were waited for; matrix products, arithmetic and copies ran while one was open for 8% of the time, Pallas kernels for 20%

profile of v3, /device:TPU:0, one launch (start us, length us, event | category | flops | bytes accessed | tf_op | source)
XLA Modules:
  0.0 163.3 jit_solution(11761084659823657655)
XLA Ops:
  0.6 1.3 fusion.6
  1.9 1.2 slice_bitcast_fusion.2
  3.1 0.0 copy-start.3
  3.1 0.0 copy-start.2
  3.1 0.0 copy-start.1
  3.1 0.8 pad_maximum_fusion.2
  3.9 3.0 %collective-permute-start.2 = (f32[9,96,96]{2,1,0:T(8,128)}, f32[9,96,96]{2,1,0:T(8,128)}, u32[]{:S(2)}, u32[]{:S(2)}) collective-permute-start(f32[9,96,96]{2,1,0:T(8,128)} %pad_maximum_fusion.2), channel_id=1, source_target_pairs={{24,0},{0,8},{8,16},{16,24},{25,1},{1,9},{9,17},{17,25},{26,2},{2,... | collective-permute-start | bytes 995336 | tf_op jit(solution)/shard_map/ppermute | solution.py:21
  7.0 0.0 copy-done.3
  7.0 0.8 pad_maximum_fusion.3
  7.8 0.0 copy-start.6
  7.8 0.0 slice-start
  7.8 0.0 collective-permute-start.3
  7.8 0.0 copy-done.1
  7.8 0.1 slice_bitcast_fusion
  7.9 0.0 copy-done.2
  7.9 0.6 copy-done.6
  8.5 0.3 slice-done
  8.8 0.2 copy.15
  8.9 0.4 copy.14
  9.3 0.0 copy-start
  9.3 1.4 pad_maximum_fusion.1
  10.8 1.5 collective-permute-start.1
  12.3 0.0 copy-done
  12.3 5.1 %fusion.1 = f32[4,4,96,256]{3,2,1,0:T(8,128)S(1)} fusion(f32[4,4,1,96,256]{4,3,2,1,0:T(8,128)S(1)} %copy-done), kind=kLoop, calls=%fused_computation.3 | loop fusion | flops 393216 | bytes 3145728 | tf_op jit(solution)/shard_map/mul | solution.py:421
  17.4 0.3 fusion.7
  17.7 0.6 collective-permute-start
  18.2 17.4 %shard_map.95 = (bf16[4,768,1536]{2,1,0:T(8,128)(2,1)}, bf16[1,768,384]{2,1,0:T(8,128)(2,1)}, bf16[1,768,384]{2,1,0:T(8,128)(2,1)}) custom-call(s32[2,48]{1,0:T(2,128)} %bitcast.56, s32[2,8]{1,0:T(2,128)} %get-tuple-element.26.refs_1_.refs_3_, s32[2,8]{1,0:T(2,128)} %get-tuple-element.25.refs_2_, s32[2,8]{1,0:T(2,128)} %get-tuple-element.26.refs_1_.refs_3_, ...), custom_call_target="tpu_custom_call" | custom-call | flops 15000000512 | bytes 60000000 | tf_op jit(solution)/shard_map/pallas_call | solution.py:132
  35.7 1.3 pad_maximum_fusion.refs_0_
  37.0 0.0 collective-permute-done.2.refs_6_
  37.0 1.3 fusion.3.refs_2_
  38.2 0.0 collective-permute-done.3.refs_7_
  38.2 1.2 fusion.2.refs_3_
  39.5 1.5 collective-permute-done.1.refs_5_
  41.0 1.2 fusion.4.refs_1_
  42.2 14.8 %shard_map.96 = (bf16[4,768,1536]{2,1,0:T(8,128)(2,1)}, bf16[1,768,384]{2,1,0:T(8,128)(2,1)}, bf16[1,768,384]{2,1,0:T(8,128)(2,1)}) custom-call(s32[2,32]{1,0:T(2,128)} %bitcast.53, s32[2,32]{1,0:T(2,128)} %fusion.4.refs_1_, s32[2,8]{1,0:T(2,128)} %fusion.3.refs_2_, s32[2,8]{1,0:T(2,128)} %fusion.2.refs_3_, f32[32,96,96]{2,1,0:T(8,128)} %bitcast.50, ...), custom_call_target="tpu_custom_call" | custom-call | flops 7500000256 | bytes 30000000 | tf_op jit(solution)/shard_map/pallas_call | solution.py:132
  57.0 0.5 collective-permute-done.refs_1_
  57.5 0.0 copy-start.4
  57.5 0.9 copy-done.4
  58.4 101.6 %shard_map.97 = (f32[4,4,1,96,256]{4,3,2,1,0:T(8,128)}, f32[7,1,256]{2,1,0:T(1,128)}) custom-call(f32[2,4,4,96,128]{4,3,2,1,0:T(8,128)} %pad_maximum_fusion.refs_0_, f32[4,4,96,128]{3,2,1,0:T(8,128)} %copy-done.4, bf16[4,768,1536]{2,1,0:T(8,128)(2,1)} %get-tuple-element.10.refs_2_, bf16[4,768,1536]{2,1,0:T(8,128)(2,1)} %get-tuple-element.11.refs_3_, ...), custom_call_target="tpu_custom_call" | custom-call | tf_op jit(solution)/shard_map/pallas_call | solution.py:371
  160.0 0.0 copy-start.5
  160.0 2.7 %copy.18 = f32[4,4,1,96,256]{4,3,2,1,0:T(8,128)} copy(f32[4,4,1,96,256]{4,3,2,1,0:T(8,128)} %get-tuple-element.29) | data formatting | bytes 3145728
  162.7 0.0 copy-done.5
  162.7 0.6 copy.19
  (4 shorter events, 0.0 us)
Async XLA Ops:
  3.1 3.9 %copy-start.3 = (f32[8,96,96]{2,1,0:T(8,128)}, f32[8,96,96]{2,1,0:T(8,128)S(1)}, u32[]{:S(2)}) copy-start(f32[8,96,96]{2,1,0:T(8,128)S(1)} %get-tuple-element.22.refs_5_) | copy-start | bytes 884740
  3.1 4.8 %copy-start.2 = (f32[8,96,96]{2,1,0:T(8,128)}, f32[8,96,96]{2,1,0:T(8,128)S(1)}, u32[]{:S(2)}) copy-start(f32[8,96,96]{2,1,0:T(8,128)S(1)} %get-tuple-element.21.refs_6_) | copy-start | bytes 884740
  3.1 4.7 %copy-start.1 = (f32[1,1,1,32,96,96]{5,4,3,2,1,0:T(8,128)S(1)}, f32[1,1,1,32,96,96]{5,4,3,2,1,0:T(8,128)}, u32[]{:S(2)}) copy-start(f32[1,1,1,32,96,96]{5,4,3,2,1,0:T(8,128)} %param.14) | copy-start | bytes 3538948
  3.9 33.0 %collective-permute-start.2 = (f32[9,96,96]{2,1,0:T(8,128)}, f32[9,96,96]{2,1,0:T(8,128)}, u32[]{:S(2)}, u32[]{:S(2)}) collective-permute-start(f32[9,96,96]{2,1,0:T(8,128)} %pad_maximum_fusion.2), channel_id=1, source_target_pairs={{24,0},{0,8},{8,16},{16,24},{25,1},{1,9},{9,17},{17,25},{26,2},{2,... | collective-permute-start | bytes 995336 | tf_op jit(solution)/shard_map/ppermute | solution.py:21
  7.8 0.7 copy-start.6
  7.8 1.0 slice-start
  7.8 30.5 %collective-permute-start.3 = (f32[9,96,96]{2,1,0:T(8,128)}, f32[9,96,96]{2,1,0:T(8,128)}, u32[]{:S(2)}, u32[]{:S(2)}) collective-permute-start(f32[9,96,96]{2,1,0:T(8,128)} %pad_maximum_fusion.3), channel_id=1, source_target_pairs={{6,0},{0,2},{2,4},{4,6},{7,1},{1,3},{3,5},{5,7},{14,8},{8,10},{10,... | collective-permute-start | bytes 995336 | tf_op jit(solution)/shard_map/ppermute | solution.py:21
  9.3 3.0 %copy-start = (f32[4,4,1,96,256]{4,3,2,1,0:T(8,128)S(1)}, f32[4,4,1,96,256]{4,3,2,1,0:T(8,128)}, u32[]{:S(2)}) copy-start(f32[4,4,1,96,256]{4,3,2,1,0:T(8,128)} %param.8) | copy-start | bytes 4718596
  10.8 30.2 %collective-permute-start.1 = (f32[25,96,128]{2,1,0:T(8,128)}, f32[25,96,128]{2,1,0:T(8,128)}, u32[]{:S(2)}, u32[]{:S(2)}) collective-permute-start(f32[25,96,128]{2,1,0:T(8,128)} %pad_maximum_fusion.1), channel_id=1, source_target_pairs={{1,0},{0,1},{3,2},{2,3},{5,4},{4,5},{7,6},{6,7},{9,8},{8,9},{11,10... | collective-permute-start | bytes 3686408 | tf_op jit(solution)/shard_map/ppermute | solution.py:21
  17.7 39.8 %collective-permute-start = (f32[4,4,96,128]{3,2,1,0:T(8,128)S(1)}, f32[4,4,96,128]{3,2,1,0:T(8,128)S(1)}, u32[]{:S(2)}, u32[]{:S(2)}) collective-permute-start(f32[4,4,96,128]{3,2,1,0:T(8,128)S(1)} %get-tuple-element.18), channel_id=1, source_target_pairs={{1,0},{0,1},{3,2},{2,3},{5,4},{4,5},{7,6},{6,7},{9,8},{8,9},{11,10... | collective-permute-start | bytes 2359304 | tf_op jit(solution)/shard_map/ppermute | solution.py:21
  57.5 0.9 copy-start.4
  160.0 2.7 %copy-start.5 = (f32[7,1,256]{2,1,0:T(1,128)S(1)}, f32[7,1,256]{2,1,0:T(1,128)}, u32[]{:S(2)}) copy-start(f32[7,1,256]{2,1,0:T(1,128)} %get-tuple-element.17) | copy-start | bytes 21508

commit v4 on v3

--- a/solution.py
+++ b/solution.py
@@ -9,7 +9,7 @@
 from jax.sharding import PartitionSpec as P
 
 CHUNKS = 2
-TOGETHER = 4
+TOGETHER = 8
 PIECES = 2
 MESH = pl.DeviceIdType.MESH
 VMEM_LIMIT = 60 * 1024 * 1024

time: 164 us -> 163 us (level)
  Pallas kernels: 134 us -> 132 us
  waiting for transfers between devices: 2.04 us -> 3.84 us
    ppermute x4, waiting for transfers between devices: 2.04 us -> 3.84 us  [passed_along(): return lax.ppermute(block, axis, route)]
    pallas_call x2, Pallas kernels: 32.2 us -> 30.4 us  [build(): pl.pallas_call(functools.partial(build_kernel, plan, counts, edge), out_s...]
  transfers between devices with their start and end apart: 4 -> 4, of which waited for: 2 -> 2; matrix products, arithmetic and copies ran while one was open for 8% -> 8% of each run, Pallas kernels for 20% -> 19%
where the time goes in v4:
time: 163 us
  Pallas kernels  132 us (81%)
  other arithmetic  14.4 us (9%)
  local copies, waits for them, and re-layouts  7.19 us (4%)
  starting transfers between devices  5.12 us (3%)
  waiting for transfers between devices  3.84 us (2%)
    pallas_call x1, Pallas kernels, recur(): pl.pallas_call(functools.partial(recur_kernel, layers, nx, ny, normalizer...  101 us
    pallas_call x2, Pallas kernels, build(): pl.pallas_call(functools.partial(build_kernel, plan, counts, edge), out_s...  30.4 us
    ppermute x4, starting transfers between devices, passed_along(): return lax.ppermute(block, axis, route)  5.12 us
    mul x1, other arithmetic, shards(): initial = math.sqrt(2.0) * jnp.cos(phases[:, :, 0])  5.07 us
    unnamed x17, local copies, waits for them, and re-layouts  4.94 us
    ppermute x4, waiting for transfers between devices, passed_along(): return lax.ppermute(block, axis, route)  3.84 us
    convert_element_type x3, other arithmetic, sent_along(): return (received, received[-1, 0:2, 0:pairs.shape[1]].astype(jnp.int32))  3.75 us
  transfers between devices with their start and end apart: 4, of which 2 were waited for; matrix products, arithmetic and copies ran while one was open for 8% of the time, Pallas kernels for 19%

profile of v4, /device:TPU:0, one launch (start us, length us, event | category | flops | bytes accessed | tf_op | source)
XLA Modules:
  0.0 162.9 jit_solution(11010350376605872831)
XLA Ops:
  0.6 1.3 fusion.6
  1.9 1.2 slice_bitcast_fusion.2
  3.1 0.0 copy-start.3
  3.1 0.0 copy-start.2
  3.1 0.0 copy-start.1
  3.1 0.8 pad_maximum_fusion.2
  3.9 3.0 %collective-permute-start.2 = (f32[9,96,96]{2,1,0:T(8,128)}, f32[9,96,96]{2,1,0:T(8,128)}, u32[]{:S(2)}, u32[]{:S(2)}) collective-permute-start(f32[9,96,96]{2,1,0:T(8,128)} %pad_maximum_fusion.2), channel_id=1, source_target_pairs={{24,0},{0,8},{8,16},{16,24},{25,1},{1,9},{9,17},{17,25},{26,2},{2,... | collective-permute-start | bytes 995336 | tf_op jit(solution)/shard_map/ppermute | solution.py:21
  7.0 0.0 copy-done.3
  7.0 0.8 pad_maximum_fusion.3
  7.8 0.0 copy-start.6
  7.8 0.0 slice-start
  7.8 0.0 collective-permute-start.3
  7.8 0.0 copy-done.1
  7.8 0.1 slice_bitcast_fusion
  7.9 0.0 copy-done.2
  7.9 0.6 copy-done.6
  8.5 0.3 slice-done
  8.8 0.2 copy.15
  8.9 0.4 copy.14
  9.3 0.0 copy-start
  9.3 1.4 pad_maximum_fusion.1
  10.8 1.5 collective-permute-start.1
  12.3 0.0 copy-done
  12.3 5.1 %fusion.1 = f32[4,4,96,256]{3,2,1,0:T(8,128)S(1)} fusion(f32[4,4,1,96,256]{4,3,2,1,0:T(8,128)S(1)} %copy-done), kind=kLoop, calls=%fused_computation.3 | loop fusion | flops 393216 | bytes 3145728 | tf_op jit(solution)/shard_map/mul | solution.py:421
  17.4 0.3 fusion.7
  17.7 0.6 collective-permute-start
  18.2 16.5 %shard_map.95 = (bf16[4,768,1536]{2,1,0:T(8,128)(2,1)}, bf16[1,768,384]{2,1,0:T(8,128)(2,1)}, bf16[1,768,384]{2,1,0:T(8,128)(2,1)}) custom-call(s32[2,48]{1,0:T(2,128)} %bitcast.56, s32[2,8]{1,0:T(2,128)} %get-tuple-element.26.refs_1_.refs_3_, s32[2,8]{1,0:T(2,128)} %get-tuple-element.25.refs_2_, s32[2,8]{1,0:T(2,128)} %get-tuple-element.26.refs_1_.refs_3_, ...), custom_call_target="tpu_custom_call" | custom-call | flops 15000000512 | bytes 60000000 | tf_op jit(solution)/shard_map/pallas_call | solution.py:132
  34.8 1.3 pad_maximum_fusion.refs_0_
  36.1 0.0 collective-permute-done.2.refs_6_
  36.1 1.3 fusion.3.refs_2_
  37.3 0.0 collective-permute-done.3.refs_7_
  37.3 1.2 fusion.2.refs_3_
  38.6 2.4 %collective-permute-done.1.refs_5_ = f32[25,96,128]{2,1,0:T(8,128)} collective-permute-done((f32[25,96,128]{2,1,0:T(8,128)}, f32[25,96,128]{2,1,0:T(8,128)}, u32[]{:S(2)}, u32[]{:S(2)}) %collective-permute-start.1) | collective-permute-done | bytes 1228832 | tf_op jit(solution)/shard_map/ppermute | solution.py:21
  41.0 1.2 fusion.4.refs_1_
  42.2 13.9 %shard_map.96 = (bf16[4,768,1536]{2,1,0:T(8,128)(2,1)}, bf16[1,768,384]{2,1,0:T(8,128)(2,1)}, bf16[1,768,384]{2,1,0:T(8,128)(2,1)}) custom-call(s32[2,32]{1,0:T(2,128)} %bitcast.53, s32[2,32]{1,0:T(2,128)} %fusion.4.refs_1_, s32[2,8]{1,0:T(2,128)} %fusion.3.refs_2_, s32[2,8]{1,0:T(2,128)} %fusion.2.refs_3_, f32[32,96,96]{2,1,0:T(8,128)} %bitcast.50, ...), custom_call_target="tpu_custom_call" | custom-call | flops 7500000256 | bytes 30000000 | tf_op jit(solution)/shard_map/pallas_call | solution.py:132
  56.1 1.4 collective-permute-done.refs_1_
  57.5 0.0 copy-start.4
  57.5 0.9 copy-done.4
  58.4 101.2 %shard_map.97 = (f32[4,4,1,96,256]{4,3,2,1,0:T(8,128)}, f32[7,1,256]{2,1,0:T(1,128)}) custom-call(f32[2,4,4,96,128]{4,3,2,1,0:T(8,128)} %pad_maximum_fusion.refs_0_, f32[4,4,96,128]{3,2,1,0:T(8,128)} %copy-done.4, bf16[4,768,1536]{2,1,0:T(8,128)(2,1)} %get-tuple-element.10.refs_2_, bf16[4,768,1536]{2,1,0:T(8,128)(2,1)} %get-tuple-element.11.refs_3_, ...), custom_call_target="tpu_custom_call" | custom-call | tf_op jit(solution)/shard_map/pallas_call | solution.py:371
  159.6 0.0 copy-start.5
  159.6 2.7 %copy.18 = f32[4,4,1,96,256]{4,3,2,1,0:T(8,128)} copy(f32[4,4,1,96,256]{4,3,2,1,0:T(8,128)} %get-tuple-element.29) | data formatting | bytes 3145728
  162.3 0.0 copy-done.5
  162.3 0.6 copy.19
  (4 shorter events, 0.0 us)
Async XLA Ops:
  3.1 3.9 %copy-start.3 = (f32[8,96,96]{2,1,0:T(8,128)}, f32[8,96,96]{2,1,0:T(8,128)S(1)}, u32[]{:S(2)}) copy-start(f32[8,96,96]{2,1,0:T(8,128)S(1)} %get-tuple-element.22.refs_5_) | copy-start | bytes 884740
  3.1 4.8 %copy-start.2 = (f32[8,96,96]{2,1,0:T(8,128)}, f32[8,96,96]{2,1,0:T(8,128)S(1)}, u32[]{:S(2)}) copy-start(f32[8,96,96]{2,1,0:T(8,128)S(1)} %get-tuple-element.21.refs_6_) | copy-start | bytes 884740
  3.1 4.7 %copy-start.1 = (f32[1,1,1,32,96,96]{5,4,3,2,1,0:T(8,128)S(1)}, f32[1,1,1,32,96,96]{5,4,3,2,1,0:T(8,128)}, u32[]{:S(2)}) copy-start(f32[1,1,1,32,96,96]{5,4,3,2,1,0:T(8,128)} %param.14) | copy-start | bytes 3538948
  3.9 32.1 %collective-permute-start.2 = (f32[9,96,96]{2,1,0:T(8,128)}, f32[9,96,96]{2,1,0:T(8,128)}, u32[]{:S(2)}, u32[]{:S(2)}) collective-permute-start(f32[9,96,96]{2,1,0:T(8,128)} %pad_maximum_fusion.2), channel_id=1, source_target_pairs={{24,0},{0,8},{8,16},{16,24},{25,1},{1,9},{9,17},{17,25},{26,2},{2,... | collective-permute-start | bytes 995336 | tf_op jit(solution)/shard_map/ppermute | solution.py:21
  7.8 0.7 copy-start.6
  7.8 1.0 slice-start
  7.8 29.6 %collective-permute-start.3 = (f32[9,96,96]{2,1,0:T(8,128)}, f32[9,96,96]{2,1,0:T(8,128)}, u32[]{:S(2)}, u32[]{:S(2)}) collective-permute-start(f32[9,96,96]{2,1,0:T(8,128)} %pad_maximum_fusion.3), channel_id=1, source_target_pairs={{6,0},{0,2},{2,4},{4,6},{7,1},{1,3},{3,5},{5,7},{14,8},{8,10},{10,... | collective-permute-start | bytes 995336 | tf_op jit(solution)/shard_map/ppermute | solution.py:21
  9.3 3.0 %copy-start = (f32[4,4,1,96,256]{4,3,2,1,0:T(8,128)S(1)}, f32[4,4,1,96,256]{4,3,2,1,0:T(8,128)}, u32[]{:S(2)}) copy-start(f32[4,4,1,96,256]{4,3,2,1,0:T(8,128)} %param.8) | copy-start | bytes 4718596
  10.8 30.2 %collective-permute-start.1 = (f32[25,96,128]{2,1,0:T(8,128)}, f32[25,96,128]{2,1,0:T(8,128)}, u32[]{:S(2)}, u32[]{:S(2)}) collective-permute-start(f32[25,96,128]{2,1,0:T(8,128)} %pad_maximum_fusion.1), channel_id=1, source_target_pairs={{1,0},{0,1},{3,2},{2,3},{5,4},{4,5},{7,6},{6,7},{9,8},{8,9},{11,10... | collective-permute-start | bytes 3686408 | tf_op jit(solution)/shard_map/ppermute | solution.py:21
  17.7 39.8 %collective-permute-start = (f32[4,4,96,128]{3,2,1,0:T(8,128)S(1)}, f32[4,4,96,128]{3,2,1,0:T(8,128)S(1)}, u32[]{:S(2)}, u32[]{:S(2)}) collective-permute-start(f32[4,4,96,128]{3,2,1,0:T(8,128)S(1)} %get-tuple-element.18), channel_id=1, source_target_pairs={{1,0},{0,1},{3,2},{2,3},{5,4},{4,5},{7,6},{6,7},{9,8},{8,9},{11,10... | collective-permute-start | bytes 2359304 | tf_op jit(solution)/shard_map/ppermute | solution.py:21
  57.5 0.9 copy-start.4
  159.6 2.7 %copy-start.5 = (f32[7,1,256]{2,1,0:T(1,128)S(1)}, f32[7,1,256]{2,1,0:T(1,128)}, u32[]{:S(2)}) copy-start(f32[7,1,256]{2,1,0:T(1,128)} %get-tuple-element.17) | copy-start | bytes 21508
